TPU v7x, 32 devices: a whole 2x2x4 slice. The times are simulated.
32 devices in a mesh: row: 4 (over x, core), col: 8 (over z, y).
Axes of the slice: x: 2, y: 2, z: 4, core: 2. Of those that a mesh axis runs over, the one named last changes fastest.
Arguments:
- amps: bfloat16 [4, 8, 16, 32768], P('row', 'col'), may hold values from -6 to 6
- source: bfloat16 [4, 8, 16, 32768], P('row', 'col'), may hold values from -6 to 6
- factors: bfloat16 [16, 1024, 1024], P(None, ('row', 'col')), may hold values from -0.09375 to 0.09375
- screen: int32 [16, 8, 8], replicated, may hold values from 0 to 1, as said below
- occ_energy: float32 [4], replicated, may hold values from -1.5 to -0.3
- vir_energy: float32 [1024], replicated, may hold values from 0.2 to 2.5
Outputs:
- new_amps: bfloat16 [4, 8, 16, 32768], P('row', 'col')
Inputs may be any that keep to these rules, and one draw needn't show every extreme that they name: screen[i * 4 + j, A, B] equals screen[j * 4 + i, B, A].
All inputs are finite; a program needn't handle non-finite values.
Results may differ from a plain program's by a relative error of at most 0.012.
Values may be sent and summed in bfloat16 or wider, within the bound.
A program may use at most 704 MiB of HBM per device.

v0:
```python
import jax
import jax.numpy as jnp
from jax import lax
from jax.sharding import PartitionSpec as P


def to_col_major(array, dim, row_count, col_count):
    old_shape = array.shape
    group_len = old_shape[dim] // (row_count * col_count)
    divided = array.reshape(
        old_shape[:dim] + (row_count, col_count, group_len) + old_shape[dim + 1 :]
    )
    return jnp.swapaxes(divided, dim, dim + 1).reshape(old_shape)


def ladder_over_aux(running, segment, left_part, right_factor):

    def step(total, factor_pair):
        left_one, right_one = factor_pair
        inner_part = jnp.einsum(
            "pcd,bd->pcb", segment, right_one, preferred_element_type=jnp.float32
        ).astype(jnp.bfloat16)
        return (
            total
            + jnp.einsum("ac,pcb->pab", left_one, inner_part, preferred_element_type=jnp.float32),
            None,
        )

    result, unused = lax.scan(step, running, (left_part, right_factor))
    return result


def shards(amps, source, factors, screen, occ_energy, vir_energy):
    row_count = lax.axis_size("row")
    col_count = lax.axis_size("col")
    row_id = lax.axis_index("row")
    col_id = lax.axis_index("col")
    pair_count = amps.shape[2]
    aux_count, group_size, virt_count = factors.shape
    a_local = col_count * group_size
    b_local = row_count * group_size
    occ_count = occ_energy.shape[0]
    block_count = screen.shape[1]
    block_size = virt_count // block_count
    a_index = row_id * a_local + jnp.arange(a_local)
    b_position = jnp.arange(b_local)
    b_index = b_position // group_size * a_local + col_id * group_size + b_position % group_size
    block_ids = jnp.arange(block_count)
    select_rows = (a_index[:, None] // block_size == block_ids[None, :]).astype(jnp.float32)
    select_cols = (b_index[:, None] // block_size == block_ids[None, :]).astype(jnp.float32)
    mask_tile = jnp.einsum("pxy,ax,by->pab", screen.astype(jnp.float32), select_rows, select_cols)
    amp_tile = amps.reshape(pair_count, a_local, b_local)
    masked = (amp_tile * mask_tile).astype(jnp.bfloat16)
    share_rows = lax.all_to_all(factors, "row", split_axis=0, concat_axis=1, tiled=True)
    col_ordered = lax.all_gather(share_rows, "col", axis=1, tiled=True)
    left_factor = to_col_major(col_ordered, 1, col_count, row_count)
    right_factor = to_col_major(col_ordered, 2, row_count, col_count)
    mine = lax.all_to_all(masked, "col", split_axis=0, concat_axis=2, tiled=True)
    initial = jnp.zeros((mine.shape[0], virt_count, virt_count), jnp.float32)
    ladder_sum = ladder_over_aux(
        initial, lax.all_gather(mine, "row", axis=1, tiled=True), left_factor, right_factor
    )
    reduced = lax.psum_scatter(
        ladder_sum.astype(jnp.bfloat16), "row", scatter_dimension=1, tiled=True
    ).astype(jnp.float32)
    ladder = lax.all_to_all(
        reduced.astype(jnp.bfloat16), "col", split_axis=2, concat_axis=0, tiled=True
    ).astype(reduced.dtype)
    resid = source.reshape(pair_count, a_local, b_local).astype(jnp.float32) + ladder
    split_tile = resid.reshape(pair_count, col_count, group_size, row_count, group_size)
    received = lax.all_to_all(
        lax.all_to_all(
            split_tile.astype(jnp.bfloat16), "row", split_axis=3, concat_axis=3, tiled=True
        ),
        "col",
        split_axis=1,
        concat_axis=1,
        tiled=True,
    ).astype(split_tile.dtype)
    swapped = received.transpose(0, 1, 4, 3, 2).reshape(occ_count, occ_count, a_local, b_local)
    swapped = swapped.transpose(1, 0, 2, 3).reshape(pair_count, a_local, b_local)
    rsym = resid + swapped
    occ_pair = (occ_energy[:, None] + occ_energy[None, :]).reshape(pair_count)
    vir_rows = lax.dynamic_slice_in_dim(vir_energy, row_id * a_local, a_local)
    vir_cols = lax.dynamic_slice_in_dim(
        vir_energy.reshape(row_count, col_count, group_size), col_id, 1, 1
    ).reshape(b_local)
    denominator = occ_pair[:, None, None] - vir_rows[None, :, None] - vir_cols[None, None, :]
    updated = mask_tile * (amp_tile.astype(jnp.float32) + rsym / denominator)
    return updated.astype(jnp.bfloat16).reshape(1, 1, pair_count, a_local * b_local)


def solution(mesh):
    in_specs = (
        P("row", "col", None, None),
        P("row", "col", None, None),
        P(None, ("row", "col"), None),
        P(),
        P(),
        P(),
    )
    out_specs = P("row", "col", None, None)
    return jax.shard_map(shards, mesh=mesh, in_specs=in_specs, out_specs=out_specs, check_vma=False)
```

profile of v0, /device:TPU:0, one launch (start us, length us, event | category | flops | bytes accessed | tf_op | source)
XLA Modules:
  0.0 1355.5 jit_solution(13820801006849876144)
XLA Ops:
  6.5 18.8 %all_to_all.55 = bf16[16,32,1024]{2,1,0:T(8,128)(2,1)S(1)} all-to-all(bf16[16,32,1024]{2,1,0:T(8,128)(2,1)} %param.10), channel_id=1, replica_groups=mesh['row'=4,'col'=8] {'row'}, dimensions={0} | all-to-all | bytes 2097152 | tf_op jit(solution)/shard_map/all_to_all | solution.py:54
  25.3 1.1 copy.87
  26.4 0.0 all-gather.3.cloned.1.call-update
  26.4 0.0 all-gather.5.cloned.1.call-start
  26.5 0.1 convert_bitcast_fusion.1
  26.7 1.7 copy.108
  28.4 1.9 copy.103
  30.4 0.1 copy.86
  30.5 2.4 fusion.22
  32.9 59.8 %all_to_all.56 = bf16[16,256,128]{1,2,0:T(8,128)(2,1)S(1)} all-to-all(bf16[16,256,128]{1,2,0:T(8,128)(2,1)} %get-tuple-element.91), channel_id=1, replica_groups=mesh['row'=4,'col'=8] {'col'}, dimensions={0} | all-to-all | bytes 2097152 | tf_op jit(solution)/shard_map/all_to_all | solution.py:58
  92.7 1.5 copy.91
  94.1 2.3 all_to_all.46
  96.5 0.0 all-gather.5.cloned.1.call-update
  96.5 0.2 reduce-scatter.4.cloned.1.call-start
  96.7 78.1 %all-gather.3.cloned.1.call-done = bf16[4,1024,1024]{2,1,0:T(8,128)(2,1)} async-done(((bf16[4,128,1024]{2,1,0:T(8,128)(2,1)}), bf16[4,1024,1024]{2,1,0:T(8,128)(2,1)}) %all-gather.3.cloned.1.call-update) | async-done | bytes 8388624 | tf_op jit(solution)/shard_map/all_gather | solution.py:55
  174.8 11.6 copy.88
  186.4 8.5 copy.89
  194.9 8.5 copy.92
  203.5 5.6 all-gather.5.cloned.1.call-done
  209.1 59.3 %while.11 = (s32[]{:T(128)}, f32[2,1024,1024]{1,2,0:T(8,128)}, bf16[4,1024,1024]{1,2,0:T(8,128)(2,1)}, bf16[2,1024,1024]{2,1,0:T(8,128)(2,1)}, bf16[4,1024,1024]{2,1,0:T(8,128)(2,1)}, /*index=5*/s32[]{:T(128)}, s32[]{:T(128)}) while((s32[]{:T(128)}, f32[2,1024,1024]{1,2,0:T(8,128)}, bf16[4,1024,1024]{1,2,0:T(8,128)(2,1)}, ...), condition=%wide.region_1.2_spmd.clone, body=%wide.region_0.1_spmd.clone.sunk | while | flops 8596226048 | bytes 25166932 | solution.py:29
  209.1 13.9 %bitcast_add_fusion.3 = f32[2,1024,1024]{1,2,0:T(8,128)} fusion(f32[2,1024,1024]{1,2,0:T(8,128)} %get-tuple-element.132, pred[]{:T(512)S(6)} %compare.26, bf16[2,1024,1024]{2,1,0:T(8,128)(2,1)} %get-tuple-element.141, bf16[4,1024,1024]{2,1,0:T(8,128)(2,1)} %get-tuple-element.142, s32[]{:T(128)} %get-tuple-element.131, ...), kind=kOutput, calls=%fused_computation.clone.1 | convolution fusion | flops 8596226048 | bytes 25166848 | tf_op jit(solution)/shard_map/while/body/eval_jaxpr/ac,pcb->pab/dot_general | solution.py:25
  223.0 15.1 %bitcast_add_fusion.3 = f32[2,1024,1024]{1,2,0:T(8,128)} fusion(f32[2,1024,1024]{1,2,0:T(8,128)} %get-tuple-element.132, pred[]{:T(512)S(6)} %compare.26, bf16[2,1024,1024]{2,1,0:T(8,128)(2,1)} %get-tuple-element.141, bf16[4,1024,1024]{2,1,0:T(8,128)(2,1)} %get-tuple-element.142, s32[]{:T(128)} %get-tuple-element.131, ...), kind=kOutput, calls=%fused_computation.clone.1 | convolution fusion | flops 8596226048 | bytes 25166848 | tf_op jit(solution)/shard_map/while/body/eval_jaxpr/ac,pcb->pab/dot_general | solution.py:25
  238.1 15.1 %bitcast_add_fusion.3 = f32[2,1024,1024]{1,2,0:T(8,128)} fusion(f32[2,1024,1024]{1,2,0:T(8,128)} %get-tuple-element.132, pred[]{:T(512)S(6)} %compare.26, bf16[2,1024,1024]{2,1,0:T(8,128)(2,1)} %get-tuple-element.141, bf16[4,1024,1024]{2,1,0:T(8,128)(2,1)} %get-tuple-element.142, s32[]{:T(128)} %get-tuple-element.131, ...), kind=kOutput, calls=%fused_computation.clone.1 | convolution fusion | flops 8596226048 | bytes 25166848 | tf_op jit(solution)/shard_map/while/body/eval_jaxpr/ac,pcb->pab/dot_general | solution.py:25
  253.2 15.1 %bitcast_add_fusion.3 = f32[2,1024,1024]{1,2,0:T(8,128)} fusion(f32[2,1024,1024]{1,2,0:T(8,128)} %get-tuple-element.132, pred[]{:T(512)S(6)} %compare.26, bf16[2,1024,1024]{2,1,0:T(8,128)(2,1)} %get-tuple-element.141, bf16[4,1024,1024]{2,1,0:T(8,128)(2,1)} %get-tuple-element.142, s32[]{:T(128)} %get-tuple-element.131, ...), kind=kOutput, calls=%fused_computation.clone.1 | convolution fusion | flops 8596226048 | bytes 25166848 | tf_op jit(solution)/shard_map/while/body/eval_jaxpr/ac,pcb->pab/dot_general | solution.py:25
  268.4 6.0 convert_element_type.93
  274.4 176.5 %copy.105 = bf16[2,1024,1024]{0,2,1:T(8,128)(2,1)} copy(bf16[2,1024,1024]{1,2,0:T(8,128)(2,1)} %convert_element_type.93) | data formatting | bytes 8388608
  450.8 486.0 %reshape.214 = bf16[1024,2048]{1,0:T(8,128)(2,1)} reshape(bf16[1024,1024,2]{2,1,0:T(8,128)(2,1)} %bitcast.27) | data formatting | bytes 8388608
  936.9 44.7 %reduce-scatter.4.cloned.1.call-done = bf16[256,2048]{1,0:T(8,128)(2,1)} async-done(((bf16[1024,2048]{1,0:T(8,128)(2,1)}), bf16[256,2048]{1,0:T(8,128)(2,1)}) %reduce-scatter.4.cloned.1.call-update) | async-done | bytes 1048592
  981.5 146.8 %reshape.215 = bf16[256,1024,2]{2,1,0:T(8,128)(2,1)} reshape(bf16[256,2048]{1,0:T(8,128)(2,1)} %reduce-scatter.4.cloned.1.call-done) | data formatting | bytes 2097152
  1128.3 59.3 %copy.106 = bf16[2,256,1024]{1,0,2:T(2,128)(2,1)} copy(bf16[2,256,1024]{0,2,1:T(8,128)(2,1)} %bitcast.28) | data formatting | bytes 2097152
  1187.6 5.5 all-to-all-start.2
  1193.1 6.5 reshape.200
  1199.6 19.2 %all-to-all-done.2 = bf16[2,256,1024]{1,0,2:T(2,128)(2,1)S(1)} async-done(((bf16[2,256,1024]{1,0,2:T(2,128)(2,1)}), bf16[2,256,1024]{1,0,2:T(2,128)(2,1)S(1)}, u32[]{:S(2)}, u32[]{:S(2)}) %all-to-all-start.2) | async-done | bytes 1048608 | tf_op jit(solution)/shard_map/all_to_all | solution.py:66
  1218.9 0.2 copy.119
  1219.1 4.3 reshape.201
  1223.4 9.2 copy.98
  1232.7 9.0 copy_bitcast_fusion.2
  1241.6 5.6 reshape.224
  1247.2 16.9 %all_to_all.57 = bf16[4,2,65536]{2,1,0:T(2,128)(2,1)S(1)} all-to-all(bf16[4,2,65536]{2,1,0:T(2,128)(2,1)S(1)} %reshape.224), channel_id=1, replica_groups=mesh['row'=4,'col'=8] {'row'}, dimensions={0} | all-to-all | bytes 2097152 | tf_op jit(solution)/shard_map/all_to_all | solution.py:72
  1264.1 3.5 reshape.225
  1267.6 9.6 copy.120
  1277.2 7.9 reshape.226
  1285.1 4.4 all-to-all-start.4
  1289.5 0.1 reshape.195
  1289.6 0.1 dynamic_slice.13
  1289.7 0.1 broadcast_add_fusion
  1289.8 0.1 add.112
  1289.9 0.1 sub.58
  1290.0 0.1 convert_bitcast_fusion.2
  1290.1 0.4 copy.109
  1290.5 1.9 copy.96
  1292.4 0.1 broadcast_subtract_fusion
  1292.5 1.5 copy.95
  1294.0 21.2 %all-to-all-done.4 = bf16[8,2,32768]{2,1,0:T(2,128)(2,1)} async-done(((bf16[8,2,32768]{2,1,0:T(2,128)(2,1)}), bf16[8,2,32768]{2,1,0:T(2,128)(2,1)}, u32[]{:S(2)}, u32[]{:S(2)}) %all-to-all-start.4) | async-done | bytes 1048608 | tf_op jit(solution)/shard_map/all_to_all | solution.py:71
  1315.2 7.0 reshape.227
  1322.3 3.4 convert_bitcast_fusion
  1325.7 9.8 copy.101
  1335.5 5.8 reshape.208
  1341.3 0.1 copy.102
  1341.5 1.4 copy-done.1
  1342.9 0.6 copy-done.2
  1343.5 3.3 fusion.23
  1346.8 0.7 copy.104
  1347.5 1.3 reshape.196
  (23 shorter events, 0.1 us)
Async XLA Ops:
  6.5 20.0 %copy-start.5 = (bf16[1,1,16,32768]{3,2,1,0:T(8,128)(2,1)S(1)}, bf16[1,1,16,32768]{3,2,1,0:T(8,128)(2,1)}, u32[]{:S(2)}) copy-start(bf16[1,1,16,32768]{3,2,1,0:T(8,128)(2,1)} %param.8) | copy-start | bytes 3145732
  6.5 168.3 %all-gather.3.cloned.1.call-start = ((), (), s32[]{:S(2)}) async-start(), calls=%async_computation.6 | async-start | bytes 9437184 | tf_op jit(solution)/shard_map/all_gather | solution.py:55
  26.4 182.6 %all-gather.5.cloned.1.call-start = ((), (), s32[]{:S(2)}) async-start(), calls=%async_computation.7 | async-start | bytes 5242880 | tf_op jit(solution)/shard_map/all_gather | solution.py:61
  26.6 3.7 copy-start.6
  30.3 63.8 %copy-start = (f32[16,256,128]{1,2,0:T(8,128)}, f32[16,256,128]{1,2,0:T(8,128)S(1)}, u32[]{:S(2)}) copy-start(f32[16,256,128]{1,2,0:T(8,128)S(1)} %copy.103) | copy-start | bytes 6291460
  96.5 885.0 %reduce-scatter.4.cloned.1.call-start = ((), (), s32[]{:S(2)}) async-start(), calls=%async_computation.8 | async-start | bytes 5242880
  1128.3 64.8 %copy-start.3 = (bf16[1,1,16,32768]{3,2,1,0:T(8,128)(2,1)S(1)}, bf16[1,1,16,32768]{3,2,1,0:T(8,128)(2,1)}, u32[]{:S(2)}) copy-start(bf16[1,1,16,32768]{3,2,1,0:T(8,128)(2,1)} %param.9) | copy-start | bytes 3145732
  1187.6 31.3 %all-to-all-start.2 = ((bf16[2,256,1024]{1,0,2:T(2,128)(2,1)}), bf16[2,256,1024]{1,0,2:T(2,128)(2,1)S(1)}, u32[]{:S(2)}, u32[]{:S(2)}) async-start(bf16[2,256,1024]{1,0,2:T(2,128)(2,1)} %copy.106), calls=%async_computation.2 | async-start | bytes 2097152 | tf_op jit(solution)/shard_map/all_to_all | solution.py:66
  1277.2 12.4 copy-start.7
  1277.2 12.5 copy-start.8
  1277.2 12.8 copy-start.4
  1285.1 30.1 %all-to-all-start.4 = ((bf16[8,2,32768]{2,1,0:T(2,128)(2,1)}), bf16[8,2,32768]{2,1,0:T(2,128)(2,1)}, u32[]{:S(2)}, u32[]{:S(2)}) async-start(bf16[8,2,32768]{2,1,0:T(2,128)(2,1)} %reshape.226), calls=%async_computation.4 | async-start | bytes 2097152 | tf_op jit(solution)/shard_map/all_to_all | solution.py:71
  1341.3 1.6 copy-start.1
  1341.3 2.2 copy-start.2
Sparse Core Ops, SparseCore 0:
  26.6 148.2 all-gather.2
  176.4 32.6 all-gather.4
  937.0 44.4 reduce-scatter.3
where the time goes:
time: 1370 us; the launch traced here: 1360 us
  local copies, waits for them, and re-layouts  984 us (72%)
  waiting for transfers between devices  169 us (12%)
  blocking collectives  95.5 us (7%)
  matrix products  61.7 us (5%)
  other arithmetic  22.1 us (2%)
    unnamed x28, local copies, waits for them, and re-layouts  897 us
    all_gather x1, waiting for transfers between devices, shards(): col_ordered = lax.all_gather(share_rows, 'col', axis=1, tiled=True)  78.1 us
    all_to_all x1, blocking collectives, shards(): lax.all_to_all(masked, 'col', split_axis=0, concat_axis=2, tiled=True)  59.8 us
    dot_general x4, matrix products, step(): jnp.einsum('ac,pcb->pab', left_one, inner_part, preferred_element_type=jn...  59.3 us
    unnamed x4, waiting for transfers between devices  44.7 us
  transfers between devices with their start and end apart: 5, of which 5 were waited for; matrix products, arithmetic and copies ran while one was open for 3% of the time, Pallas kernels for 0%

commit v1 on v0

--- a/solution.py
+++ b/solution.py
@@ -1,7 +1,304 @@
+import functools
+
 import jax
 import jax.numpy as jnp
 from jax import lax
+from jax.experimental import pallas as pl
+from jax.experimental.pallas import tpu as pltpu
 from jax.sharding import PartitionSpec as P
+
+VMEM = pltpu.VMEM
+LANES = 128
+
+
+def pair_table(occ_count):
+    table = []
+    for i in range(occ_count):
+        for j in range(i + 1, occ_count):
+            table.append((i * occ_count + j, j * occ_count + i))
+    for i in range(0, occ_count, 2):
+        table.append((i * occ_count + i, (i + 1) * occ_count + i + 1))
+    return table
+
+
+def whole(count):
+    return [pl.BlockSpec(memory_space=VMEM)] * count
+
+
+def pack_kernel(table, amps_ref, source_ref, mask_ref, tm_ref, s_ref, rows):
+    pair_count, a_local = rows.shape[0], rows.shape[1]
+    groups, group = tm_ref.shape[2], tm_ref.shape[3]
+    half_len = a_local // mask_ref.shape[0]
+
+    def turn(in_ref, out_ref, masked):
+        for half in range(mask_ref.shape[0]):
+
+            @pl.loop(0, half_len, unroll=8)
+            def _(step):
+                x = half * half_len + step
+                one = in_ref[:, pl.ds(pl.multiple_of(x * LANES, LANES), LANES)].astype(jnp.float32)
+                if masked:
+                    one = one * mask_ref[half]
+                rows[:, x, :] = one
+
+        for dest, pairs in enumerate(table):
+            for slot, pair in enumerate(pairs):
+                turned = rows[pair].T.astype(jnp.bfloat16)
+                out_ref[dest, slot] = turned.reshape(groups, group, a_local)
+
+    turn(amps_ref, tm_ref, True)
+    turn(source_ref, s_ref, False)
+
+
+def ladder_kernel(last, *refs):
+    if last:
+        t_ref, b_ref, prior_ref, out_ref, total, t_all, b_all, inner, t_sem, b_sem, p_sem = refs
+    else:
+        t_ref, b_ref, out_ref, t_all, b_all, inner, t_sem, b_sem = refs
+        total = out_ref
+    row_count, col_count, slots = t_ref.shape[0], t_ref.shape[1], t_ref.shape[2]
+    a_local = t_ref.shape[5]
+    q_count = b_ref.shape[2]
+    virt = b_ref.shape[4]
+    block = 512 if virt % 512 == 0 else virt
+    blocks = virt // block
+    rows_per = block // (virt // row_count)
+
+    b_copies = [
+        [
+            pltpu.make_async_copy(b_ref.at[c, :, q], b_all.at[q, :, c], b_sem.at[q, c])
+            for c in range(col_count)
+        ]
+        for q in range(q_count)
+    ]
+    t_copies = [
+        pltpu.make_async_copy(
+            t_ref.at[r, c, p],
+            t_all.at[p, :, c, :, pl.ds(r * a_local, a_local)],
+            t_sem.at[r, c, p],
+        )
+        for p in range(slots)
+        for c in range(col_count)
+        for r in range(row_count)
+    ]
+    for copy in b_copies[0] + t_copies:
+        copy.start()
+    for some in b_copies[1:]:
+        for copy in some:
+            copy.start()
+    if last:
+        prior_copy = pltpu.make_async_copy(prior_ref, total, p_sem)
+        prior_copy.start()
+    for copy in t_copies:
+        copy.wait()
+
+    for q in range(q_count):
+        for copy in b_copies[q]:
+            copy.wait()
+        if q == 0 and last:
+            prior_copy.wait()
+        for p in range(slots):
+
+            @pl.loop(0, blocks * blocks)
+            def _(step):
+                m, n = step // blocks, step % blocks
+                left = b_all[q, pl.ds(m * rows_per, rows_per)].reshape(block, virt)
+                cols = pl.ds(pl.multiple_of(n * block, block), block)
+                right = t_all[p, :, :, :, cols].reshape(virt, block)
+                inner[pl.ds(pl.multiple_of(m * block, block), block), cols] = jnp.dot(
+                    left, right, preferred_element_type=jnp.float32
+                ).astype(jnp.bfloat16)
+
+            @pl.loop(0, blocks * blocks)
+            def _(step):
+                m, n = step // blocks, step % blocks
+                some = pl.ds(pl.multiple_of(m * block, block), block)
+                cols = pl.ds(pl.multiple_of(n * block, block), block)
+                right = b_all[q, pl.ds(n * rows_per, rows_per)].reshape(block, virt)
+                part = lax.dot_general(
+                    inner[some, :],
+                    right,
+                    (((1,), (1,)), ((), ())),
+                    preferred_element_type=jnp.float32,
+                )
+                if q > 0 or last:
+                    part = part + total[p, some, cols]
+                if last and q == q_count - 1:
+                    for k in range(rows_per):
+                        out_ref[n * rows_per + k, p, some, :] = part[
+                            :, k * a_local : (k + 1) * a_local
+                        ].astype(jnp.bfloat16)
+                else:
+                    total[p, some, cols] = part
+
+
+def resid_kernel(ladder_ref, s_ref, resid_ref, swap_ref):
+    col_count, slots, row_count, group, a_local = s_ref.shape
+    for p in range(slots):
+        for y in range(row_count):
+            for c in range(col_count):
+                some = pl.ds(y * a_local + c * group, group)
+                resid_ref[p, some, :] = s_ref[c, p, y].astype(jnp.float32) + ladder_ref[
+                    p, some, :
+                ].astype(jnp.float32)
+            swap_ref[y, p] = resid_ref[p, pl.ds(y * a_local, a_local), :].T.astype(jnp.bfloat16)
+
+
+def add_kernel(diagonal_from, resid_ref, swap_ref, out_ref):
+    col_count, slots, row_count, group, a_local = out_ref.shape
+    flip = (lax.axis_index("col") < diagonal_from).astype(jnp.int32)
+    for p in range(slots):
+        partner = p * (1 - flip) + (slots - 1 - p) * flip
+        for y in range(row_count):
+            for c in range(col_count):
+                some = pl.ds(y * a_local + c * group, group)
+                other = swap_ref[y, partner, pl.ds(c * group, group), :]
+                both = resid_ref[p, some, :] + other.astype(jnp.float32)
+                out_ref[c, p, y] = both.astype(jnp.bfloat16)
+
+
+def update_kernel(table, amps_ref, rsym_ref, mask_ref, occ_ref, vir_b_ref, vir_a_ref, out_ref, rows):
+    pair_count, a_local = rows.shape[0], rows.shape[1]
+    half_len = a_local // mask_ref.shape[0]
+    for owner, pairs in enumerate(table):
+        for slot, pair in enumerate(pairs):
+            one = rsym_ref[owner, slot].reshape(LANES, a_local).astype(jnp.float32)
+            rows[pair] = one.T
+    known = occ_ref[...] - vir_b_ref[...]
+    for half in range(mask_ref.shape[0]):
+
+        @pl.loop(0, half_len, unroll=8)
+        def _(step):
+            x = half * half_len + step
+            lanes = pl.ds(pl.multiple_of(x * LANES, LANES), LANES)
+            denom = known - vir_a_ref[x]
+            new = mask_ref[half] * (amps_ref[:, lanes].astype(jnp.float32) + rows[:, x, :] / denom)
+            out_ref[:, lanes] = new.astype(jnp.bfloat16)
+
+
+def params(limit=56):
+    return pltpu.CompilerParams(vmem_limit_bytes=limit * 1024 * 1024)
+
+
+def fast_shards(amps, source, factors, screen, occ_energy, vir_energy):
+    row_count = lax.axis_size("row")
+    col_count = lax.axis_size("col")
+    row_id = lax.axis_index("row")
+    col_id = lax.axis_index("col")
+    pair_count = amps.shape[2]
+    aux_count, group, virt = factors.shape
+    a_local = col_count * group
+    b_local = row_count * group
+    occ_count = occ_energy.shape[0]
+    block_count = screen.shape[1]
+    block_size = virt // block_count
+    halves = a_local // block_size
+    per_y = block_count // row_count
+    slots = pair_count // col_count
+    share = aux_count // row_count
+    table = pair_table(occ_count)
+    bf16, f32 = jnp.bfloat16, jnp.float32
+
+    amps = amps.reshape(pair_count, a_local * b_local)
+    source = source.reshape(pair_count, a_local * b_local)
+    mine = lax.dynamic_slice_in_dim(screen, row_id * halves, halves, 1)
+    mine = mine.reshape(pair_count, halves, row_count, per_y)
+    mine = lax.dynamic_slice_in_dim(mine, col_id * group // block_size, 1, 3)
+    mask = jnp.broadcast_to(
+        mine.transpose(1, 0, 2, 3).astype(f32), (halves, pair_count, row_count, group)
+    ).reshape(halves, pair_count, b_local)
+    occ_pair = (occ_energy[:, None] + occ_energy[None, :]).reshape(pair_count, 1)
+    vir_a = lax.dynamic_slice_in_dim(vir_energy, row_id * a_local, a_local)
+    vir_b = lax.dynamic_slice_in_dim(
+        vir_energy.reshape(row_count, col_count, group), col_id, 1, 1
+    ).reshape(1, b_local)
+
+    chunks = 2
+    per_chunk = share // chunks
+    by_share = factors.reshape(row_count, chunks, per_chunk, group, virt)
+    gathered = []
+    for k in range(chunks):
+        rows_of = lax.all_to_all(by_share[:, k], "row", split_axis=0, concat_axis=0, tiled=True)
+        gathered.append(lax.all_gather(rows_of, "col", axis=0))
+
+    block = (col_count, slots, row_count, group, a_local)
+    tm_blocks, s_blocks = pl.pallas_call(
+        functools.partial(pack_kernel, table),
+        out_shape=[jax.ShapeDtypeStruct(block, bf16)] * 2,
+        in_specs=whole(3),
+        out_specs=whole(2),
+        scratch_shapes=[VMEM((pair_count, a_local, LANES), f32)],
+        compiler_params=params(),
+        name="pack_tiles",
+    )(amps, source, mask)
+    tm_mine = lax.all_to_all(tm_blocks, "col", split_axis=0, concat_axis=0, tiled=True)
+    s_mine = lax.all_to_all(s_blocks, "col", split_axis=0, concat_axis=0, tiled=True)
+    tm_all = lax.all_gather(tm_mine, "row", axis=0)
+
+    flops = 4 * per_chunk * slots * virt**3
+    prior = None
+    for k in range(chunks):
+        last = k == chunks - 1
+        operands = [tm_all, gathered[k]] + ([prior] if last else [])
+        total = (slots, virt, virt)
+        prior = pl.pallas_call(
+            functools.partial(ladder_kernel, last),
+            out_shape=(
+                jax.ShapeDtypeStruct((row_count, slots, virt, a_local), bf16)
+                if last
+                else jax.ShapeDtypeStruct(total, f32)
+            ),
+            in_specs=[pl.BlockSpec(memory_space=pl.ANY)] * len(operands),
+            out_specs=pl.BlockSpec(memory_space=VMEM),
+            scratch_shapes=([VMEM(total, f32)] if last else [])
+            + [
+                VMEM((slots, row_count, col_count, group, virt), bf16),
+                VMEM((per_chunk, row_count, col_count, group, virt), bf16),
+                VMEM((virt, virt), bf16),
+                pltpu.SemaphoreType.DMA((row_count, col_count, slots)),
+                pltpu.SemaphoreType.DMA((per_chunk, col_count)),
+            ]
+            + ([pltpu.SemaphoreType.DMA] if last else []),
+            compiler_params=params(),
+            cost_estimate=pl.CostEstimate(
+                flops=flops, bytes_accessed=16 * 1024 * 1024, transcendentals=0
+            ),
+            name="ladder_end" if last else "ladder_begin",
+        )(*operands)
+
+    ladder = lax.psum_scatter(prior, "row", scatter_dimension=0, tiled=True)
+    ladder = ladder.reshape(slots, virt, a_local)
+    resid, swap = pl.pallas_call(
+        resid_kernel,
+        out_shape=[
+            jax.ShapeDtypeStruct((slots, virt, a_local), f32),
+            jax.ShapeDtypeStruct((row_count, slots, a_local, a_local), bf16),
+        ],
+        in_specs=whole(2),
+        out_specs=whole(2),
+        compiler_params=params(),
+        name="resid",
+    )(ladder, s_mine)
+    swapped = lax.all_to_all(swap, "row", split_axis=0, concat_axis=0, tiled=True)
+    rsym = pl.pallas_call(
+        functools.partial(add_kernel, occ_count * (occ_count - 1) // 2),
+        out_shape=jax.ShapeDtypeStruct(block, bf16),
+        in_specs=whole(2),
+        out_specs=whole(1)[0],
+        compiler_params=params(),
+        name="add_swapped",
+    )(resid, swapped)
+    rsym = lax.all_to_all(rsym, "col", split_axis=0, concat_axis=0, tiled=True)
+    new = pl.pallas_call(
+        functools.partial(update_kernel, table),
+        out_shape=jax.ShapeDtypeStruct((pair_count, a_local * b_local), bf16),
+        in_specs=whole(5) + [pl.BlockSpec(memory_space=pltpu.SMEM)],
+        out_specs=whole(1)[0],
+        scratch_shapes=[VMEM((pair_count, a_local, LANES), f32)],
+        compiler_params=params(),
+        name="update",
+    )(amps, rsym, mask, occ_pair, vir_b, vir_a)
+    return new.reshape(1, 1, pair_count, a_local * b_local)
 
 
 def to_col_major(array, dim, row_count, col_count):
@@ -90,6 +387,27 @@
     return updated.astype(jnp.bfloat16).reshape(1, 1, pair_count, a_local * b_local)
 
 
+def fits(amps, factors, screen, occ_energy, row_count, col_count):
+    aux_count, rows, virt = factors.shape
+    group = rows // (row_count * col_count)
+    a_local, b_local = col_count * group, row_count * group
+    block_size = virt // screen.shape[1]
+    occ_count = occ_energy.shape[0]
+    return (
+        group % 16 == 0
+        and b_local == LANES
+        and a_local % LANES == 0
+        and block_size % group == 0
+        and a_local % block_size == 0
+        and occ_count % 2 == 0
+        and 2 * col_count == occ_count * occ_count
+        and amps.shape[2] == occ_count * occ_count
+        and aux_count % (2 * row_count) == 0
+        and virt % 512 == 0
+        and 512 % a_local == 0
+    )
+
+
 def solution(mesh):
     in_specs = (
         P("row", "col", None, None),
@@ -100,4 +418,13 @@
         P(),
     )
     out_specs = P("row", "col", None, None)
-    return jax.shard_map(shards, mesh=mesh, in_specs=in_specs, out_specs=out_specs, check_vma=False)
+    row_count, col_count = mesh.shape["row"], mesh.shape["col"]
+
+    def run(amps, source, factors, screen, occ_energy, vir_energy):
+        fast = fits(amps, factors, screen, occ_energy, row_count, col_count)
+        body = fast_shards if fast else shards
+        return jax.shard_map(
+            body, mesh=mesh, in_specs=in_specs, out_specs=out_specs, check_vma=False
+        )(amps, source, factors, screen, occ_energy, vir_energy)
+
+    return run

time: 1370 us -> 367 us (0.27); the launches traced: 1360 us -> 367 us
  local copies, waits for them, and re-layouts: 984 us -> 6.38 us
  Pallas kernels: 0 us -> 80 us
  matrix products: 61.7 us -> 0 us
  waiting for transfers between devices: 169 us -> 144 us
  other arithmetic: 22.1 us -> 0.08 us
  blocking collectives: 95.5 us -> 117 us
    unnamed x28 -> x10, local copies, waits for them, and re-layouts: 897 us -> 2.18 us
    pallas_call x0 -> x6, Pallas kernels: none -> 80 us  [the longest x2 62 us: fast_shards(): pl.pallas_call(functools.partial(ladder_kernel, last), out_shape=jax.Shap...]
    dot_general x5 -> x0, matrix products: 61.7 us -> none  [the longest x4 59.3 us: step(): jnp.einsum('ac,pcb->pab', left_one, inner_part, preferred_element_type=jn...]
    unnamed x4, waiting for transfers between devices: 44.7 us -> 0.07 us
    convert_element_type x9 -> x0, local copies, waits for them, and re-layouts: 26.4 us -> none  [the longest x4 15.3 us: shards(): ladder = lax.all_to_all(reduced.astype(jnp.bfloat16), 'col', split_axis=2...]
    all_gather x2 -> x3, waiting for transfers between devices: 83.7 us -> 108 us  [the longest x2 73.3 us: fast_shards(): gathered.append(lax.all_gather(rows_of, 'col', axis=0))]
    all_to_all x3 -> x5, blocking collectives: 95.5 us -> 117 us  [the longest x1 44.7 us: fast_shards(): lax.all_to_all(tm_blocks, 'col', split_axis=0, concat_axis=0, tiled=True)]
    transpose x2 -> x0, local copies, waits for them, and re-layouts: 17.1 us -> none  [to_col_major(): return jnp.swapaxes(divided, dim, dim + 1).reshape(old_shape)]
  transfers between devices with their start and end apart: 5 -> 5, of which waited for: 5 -> 5; matrix products, arithmetic and copies ran while one was open for 3% -> 1% of each run, Pallas kernels for 0% -> 10%
where the time goes in v1:
time: 367 us
  waiting for transfers between devices  144 us (39%)
  blocking collectives  117 us (32%)
  Pallas kernels  80 us (22%)
  between operations  13.2 us (4%)
  local copies, waits for them, and re-layouts  6.38 us (2%)
  starting transfers between devices  5.65 us (2%)
    all_gather x2, waiting for transfers between devices, fast_shards(): gathered.append(lax.all_gather(rows_of, 'col', axis=0))  73.3 us
    pallas_call x2, Pallas kernels, fast_shards(): pl.pallas_call(functools.partial(ladder_kernel, last), out_shape=jax.Shap...  62 us
    all_to_all x1, blocking collectives, fast_shards(): lax.all_to_all(tm_blocks, 'col', split_axis=0, concat_axis=0, tiled=True)  44.7 us
    all_gather x1, waiting for transfers between devices, fast_shards(): tm_all = lax.all_gather(tm_mine, 'row', axis=0)  34.3 us
    all_to_all x1, blocking collectives, fast_shards(): lax.all_to_all(s_blocks, 'col', split_axis=0, concat_axis=0, tiled=True)  28.7 us
    all_to_all x2, blocking collectives, fast_shards(): lax.all_to_all(by_share[:, k], 'row', split_axis=0, concat_axis=0, tiled=...  24.9 us
    all_to_all x1, waiting for transfers between devices, fast_shards(): rsym = lax.all_to_all(rsym, 'col', split_axis=0, concat_axis=0, tiled=True)  23.5 us
    all_to_all x1, blocking collectives, fast_shards(): lax.all_to_all(swap, 'row', split_axis=0, concat_axis=0, tiled=True)  18.9 us
  transfers between devices with their start and end apart: 5, of which 5 were waited for; matrix products, arithmetic and copies ran while one was open for 1% of the time, Pallas kernels for 10%

profile of v1, /device:TPU:0, one launch (start us, length us, event | category | flops | bytes accessed | tf_op | source)
XLA Modules:
  0.0 366.7 jit_solution(12049783906115455989)
XLA Ops:
  6.5 0.0 copy-start
  6.5 0.0 all-gather.11.cloned.1.call-start
  6.5 1.3 slice_bitcast_fusion
  7.8 13.0 %all_to_all.30 = bf16[4,2,32,1024]{3,2,1,0:T(8,128)(2,1)} all-to-all(bf16[4,2,32,1024]{3,2,1,0:T(8,128)(2,1)S(1)} %get-tuple-element.13), channel_id=1, replica_groups=mesh['row'=4,'col'=8] {'row'}, dimensions={0} | all-to-all | bytes 1048576 | tf_op jit(solution)/shard_map/all_to_all | solution.py:221
  20.8 0.0 all-gather.11.cloned.1.call-update
  20.8 0.0 all-gather.7.cloned.1.call-start
  20.9 0.0 copy-done
  21.0 0.1 copy.17
  21.0 0.1 broadcast_in_dim.10
  21.1 0.7 reshape.55.mask_ref
  21.8 6.8 %pack_tiles.1 = (bf16[8,2,4,32,256]{4,3,2,1,0:T(8,128)(2,1)}, bf16[8,2,4,32,256]{4,3,2,1,0:T(8,128)(2,1)}) custom-call(bf16[16,32768]{1,0:T(8,128)(2,1)} %bitcast.16, bf16[16,32768]{1,0:T(8,128)(2,1)} %bitcast.19, f32[2,16,128]{2,1,0:T(8,128)} %reshape.55.mask_ref), custom_call_target="tpu_custom_call" | custom-call | tf_op jit(solution)/shard_map/pack_tiles/pallas_call | solution.py:225
  28.6 44.7 %all_to_all.31 = bf16[8,2,4,32,256]{4,3,2,1,0:T(8,128)(2,1)} all-to-all(bf16[8,2,4,32,256]{4,3,2,1,0:T(8,128)(2,1)} %get-tuple-element.9), channel_id=1, replica_groups=mesh['row'=4,'col'=8] {'col'}, dimensions={0} | all-to-all | bytes 2097152 | tf_op jit(solution)/shard_map/all_to_all | solution.py:234
  73.3 0.0 all-gather.7.cloned.1.call-update
  73.3 0.0 all-gather.9.cloned.1.call-start
  73.4 12.0 %all_to_all.32 = bf16[4,2,32,1024]{3,2,1,0:T(8,128)(2,1)} all-to-all(bf16[4,2,32,1024]{3,2,1,0:T(8,128)(2,1)S(1)} %get-tuple-element.14), channel_id=1, replica_groups=mesh['row'=4,'col'=8] {'row'}, dimensions={0} | all-to-all | bytes 1048576 | tf_op jit(solution)/shard_map/all_to_all | solution.py:221
  85.3 0.0 all-gather.9.cloned.1.call-update
  85.4 0.0 reduce-scatter.2.cloned.1.call-start
  85.4 27.7 %all-gather.11.cloned.1.call-done = bf16[32,2,32,1024]{3,2,1,0:T(8,128)(2,1)} async-done(((bf16[4,2,32,1024]{3,2,1,0:T(8,128)(2,1)}), bf16[32,2,32,1024]{3,2,1,0:T(8,128)(2,1)}) %all-gather.11.cloned.1.call-update) | async-done | bytes 4194320 | tf_op jit(solution)/shard_map/all_gather | solution.py:222
  113.1 34.3 %all-gather.7.cloned.1.call-done = bf16[32,2,4,32,256]{4,3,2,1,0:T(8,128)(2,1)} async-done(((bf16[8,2,4,32,256]{4,3,2,1,0:T(8,128)(2,1)}), bf16[32,2,4,32,256]{4,3,2,1,0:T(8,128)(2,1)}) %all-gather.7.cloned.1.call-update) | async-done | bytes 4194320 | tf_op jit(solution)/shard_map/all_gather | solution.py:236
  147.5 30.0 %ladder_begin.1.refs_2_ = f32[2,1024,1024]{2,1,0:T(8,128)} custom-call(bf16[4,8,2,4,32,256]{5,4,3,2,1,0:T(8,128)(2,1)} %bitcast.24, bf16[8,4,2,32,1024]{4,3,2,1,0:T(8,128)(2,1)} %bitcast.23), custom_call_target="tpu_custom_call" | custom-call | flops 17179869184 | bytes 16777216 | tf_op jit(solution)/shard_map/ladder_begin/pallas_call | solution.py:244
  177.5 45.6 %all-gather.9.cloned.1.call-done = bf16[32,2,32,1024]{3,2,1,0:T(8,128)(2,1)} async-done(((bf16[4,2,32,1024]{3,2,1,0:T(8,128)(2,1)}), bf16[32,2,32,1024]{3,2,1,0:T(8,128)(2,1)}) %all-gather.9.cloned.1.call-update) | async-done | bytes 4194320 | tf_op jit(solution)/shard_map/all_gather | solution.py:222
  223.0 32.0 %ladder_end.1 = bf16[4,2,1024,256]{3,2,1,0:T(8,128)(2,1)} custom-call(bf16[4,8,2,4,32,256]{5,4,3,2,1,0:T(8,128)(2,1)} %bitcast.25, bf16[8,4,2,32,1024]{4,3,2,1,0:T(8,128)(2,1)} %bitcast.26, f32[2,1024,1024]{2,1,0:T(8,128)} %ladder_begin.1.refs_2_), custom_call_target="tpu_custom_call" | custom-call | flops 17179869184 | bytes 16777216 | tf_op jit(solution)/shard_map/ladder_end/pallas_call | solution.py:244
  255.0 0.0 copy-start.2
  255.0 0.0 reduce-scatter.2.cloned.1.call-update
  255.1 1.2 copy-done.2
  256.2 28.7 %all_to_all.33.s_ref = bf16[8,2,4,32,256]{4,3,2,1,0:T(8,128)(2,1)} all-to-all(bf16[8,2,4,32,256]{4,3,2,1,0:T(8,128)(2,1)S(1)} %copy-done.2), channel_id=1, replica_groups=mesh['row'=4,'col'=8] {'col'}, dimensions={0} | all-to-all | bytes 2097152 | tf_op jit(solution)/shard_map/all_to_all | solution.py:235
  285.0 13.0 %reduce-scatter.2.cloned.1.call-done = bf16[1,2,1024,256]{3,2,1,0:T(8,128)(2,1)} async-done(((bf16[4,2,1024,256]{3,2,1,0:T(8,128)(2,1)}), bf16[1,2,1024,256]{3,2,1,0:T(8,128)(2,1)}) %reduce-scatter.2.cloned.1.call-update) | async-done | bytes 1048592 | tf_op jit(solution)/shard_map/reduce_scatter | solution.py:269
  298.0 3.5 resid.1
  301.5 0.0 copy-start.3
  301.5 0.0 copy-start.4
  301.5 18.9 %all_to_all.34.swap_ref = bf16[4,2,256,256]{3,2,1,0:T(8,128)(2,1)} all-to-all(bf16[4,2,256,256]{3,2,1,0:T(8,128)(2,1)} %get-tuple-element.12), channel_id=1, replica_groups=mesh['row'=4,'col'=8] {'row'}, dimensions={0} | all-to-all | bytes 2097152 | tf_op jit(solution)/shard_map/all_to_all | solution.py:282
  320.4 3.0 add_swapped.1
  323.4 5.5 %all-to-all-start.5 = ((bf16[8,2,4,32,256]{4,3,2,1,0:T(8,128)(2,1)}), bf16[8,2,4,32,256]{4,3,2,1,0:T(8,128)(2,1)S(1)}, u32[]{:S(2)}, u32[]{:S(2)}) async-start(bf16[8,2,4,32,256]{4,3,2,1,0:T(8,128)(2,1)} %add_swapped.1), calls=%async_computation.6 | async-start | bytes 2097152 | tf_op jit(solution)/shard_map/all_to_all | solution.py:291
  328.9 0.0 copy-done.3
  328.9 0.1 reshape.58
  329.0 0.6 reshape.59.vir_b_ref
  329.6 0.6 dynamic_slice.15.vir_a_ref
  330.3 0.0 copy-done.4
  330.3 0.1 broadcast_add_fusion
  330.4 0.7 add.46.occ_ref
  331.0 23.5 %all-to-all-done.5.rsym_ref = bf16[8,2,4,32,256]{4,3,2,1,0:T(8,128)(2,1)S(1)} async-done(((bf16[8,2,4,32,256]{4,3,2,1,0:T(8,128)(2,1)}), bf16[8,2,4,32,256]{4,3,2,1,0:T(8,128)(2,1)S(1)}, u32[]{:S(2)}, u32[]{:S(2)}) %all-to-all-start.5) | async-done | bytes 1048608 | tf_op jit(solution)/shard_map/all_to_all | solution.py:291
  354.5 0.0 copy-start.1
  354.5 1.0 copy-done.1
  355.5 4.7 %update.1 = bf16[16,32768]{1,0:T(8,128)(2,1)} custom-call(bf16[16,32768]{1,0:T(8,128)(2,1)} %bitcast.17, bf16[8,2,4,32,256]{4,3,2,1,0:T(8,128)(2,1)} %copy-done.1, f32[2,16,128]{2,1,0:T(8,128)} %reshape.55.mask_ref, f32[16,1]{1,0:T(8,128)} %add.46.occ_ref, f32[1,128]{1,0:T(1,128)} %reshape.59.vir_b_ref, f32[256]{0:T(256)} %dynamic_slice.15.vir_a_ref), custom_call_target="tpu_custom_call" | custom-call | tf_op jit(solution)/shard_map/update/pallas_call | solution.py:292
  (3 shorter events, 0.0 us)
Async XLA Ops:
  6.5 14.4 %copy-start = (s32[16,8,8]{0,2,1:T(8,128)S(1)}, s32[16,8,8]{0,2,1:T(8,128)}, u32[]{:S(2)}) copy-start(s32[16,8,8]{0,2,1:T(8,128)} %param.9) | copy-start | bytes 12292
  6.5 106.6 %all-gather.11.cloned.1.call-start = ((), (), s32[]{:S(2)}) async-start(), calls=%async_computation.10 | async-start | bytes 4718592 | tf_op jit(solution)/shard_map/all_gather | solution.py:222
  20.8 126.6 %all-gather.7.cloned.1.call-start = ((), (), s32[]{:S(2)}) async-start(), calls=%async_computation.8 | async-start | bytes 5242880 | tf_op jit(solution)/shard_map/all_gather | solution.py:236
  73.3 149.7 %all-gather.9.cloned.1.call-start = ((), (), s32[]{:S(2)}) async-start(), calls=%async_computation.9 | async-start | bytes 4718592 | tf_op jit(solution)/shard_map/all_gather | solution.py:222
  85.4 212.6 %reduce-scatter.2.cloned.1.call-start = ((), (), s32[]{:S(2)}) async-start(), calls=%async_computation.7 | async-start | bytes 5242880 | tf_op jit(solution)/shard_map/reduce_scatter | solution.py:269
  255.0 1.2 copy-start.2
  301.5 27.4 %copy-start.3 = (f32[1024]{0:T(1024)S(1)}, f32[1024]{0:T(1024)}, u32[]{:S(2)}) copy-start(f32[1024]{0:T(1024)} %param.11) | copy-start | bytes 12292
  301.5 28.8 %copy-start.4 = (f32[4]{0:T(128)S(1)}, f32[4]{0:T(128)}, u32[]{:S(2)}) copy-start(f32[4]{0:T(128)} %param.10) | copy-start | bytes 52
  323.4 31.1 %all-to-all-start.5 = ((bf16[8,2,4,32,256]{4,3,2,1,0:T(8,128)(2,1)}), bf16[8,2,4,32,256]{4,3,2,1,0:T(8,128)(2,1)S(1)}, u32[]{:S(2)}, u32[]{:S(2)}) async-start(bf16[8,2,4,32,256]{4,3,2,1,0:T(8,128)(2,1)} %add_swapped.1), calls=%async_computation.6 | async-start | bytes 2097152 | tf_op jit(solution)/shard_map/all_to_all | solution.py:291
  354.5 1.0 copy-start.1
Sparse Core Ops, SparseCore 0:
  21.0 92.1 all-gather.10
  114.7 32.7 all-gather.6
  149.6 73.3 all-gather.8
  255.2 42.7 reduce-scatter.1

commit v2 on v1

--- a/solution.py
+++ b/solution.py
@@ -50,64 +50,195 @@
     turn(source_ref, s_ref, False)
 
 
-def ladder_kernel(last, *refs):
-    if last:
-        t_ref, b_ref, prior_ref, out_ref, total, t_all, b_all, inner, t_sem, b_sem, p_sem = refs
-    else:
-        t_ref, b_ref, out_ref, t_all, b_all, inner, t_sem, b_sem = refs
-        total = out_ref
-    row_count, col_count, slots = t_ref.shape[0], t_ref.shape[1], t_ref.shape[2]
-    a_local = t_ref.shape[5]
-    q_count = b_ref.shape[2]
-    virt = b_ref.shape[4]
-    block = 512 if virt % 512 == 0 else virt
-    blocks = virt // block
-    rows_per = block // (virt // row_count)
-
-    b_copies = [
-        [
-            pltpu.make_async_copy(b_ref.at[c, :, q], b_all.at[q, :, c], b_sem.at[q, c])
-            for c in range(col_count)
-        ]
+def ring_column(position, count):
+    position = (position + count) % count
+    back = position // (count // 2)
+    return (1 - back) * 2 * position + back * (2 * (count - 1 - position) + 1)
+
+
+def ladder_kernel(
+    tm_ref,
+    factors_ref,
+    out_ref,
+    t_all,
+    b_all,
+    inner,
+    total,
+    near_sem,
+    share_send,
+    share_recv,
+    tile_send,
+    tile_recv,
+    slab_send,
+    slab_recv,
+    ring_send,
+    ring_recv,
+):
+    q_count, row_count, col_count, group, virt = b_all.shape
+    slots, a_local = t_all.shape[1], t_all.shape[5]
+    row, col = lax.axis_index("row"), lax.axis_index("col")
+    sibling = row + 1 - 2 * (row % 2)
+    across = (row + 2) % row_count
+    place = (col // 2) * (1 - col % 2) + (col_count - 1 - col // 2) * (col % 2)
+    half_rows = row_count // 2
+
+    def remote(source, dest, send_sem, recv_sem, device):
+        return pltpu.make_async_remote_copy(
+            src_ref=source,
+            dst_ref=dest,
+            send_sem=send_sem,
+            recv_sem=recv_sem,
+            device_id=device,
+            device_id_type=pl.DeviceIdType.MESH,
+        )
+
+    barrier = pltpu.get_barrier_semaphore()
+    for step in range(1, row_count):
+        pl.semaphore_signal(
+            barrier,
+            inc=1,
+            device_id={"row": (row + step) % row_count},
+            device_id_type=pl.DeviceIdType.MESH,
+        )
+    for step in range(1, col_count):
+        pl.semaphore_signal(
+            barrier,
+            inc=1,
+            device_id={"col": (col + step) % col_count},
+            device_id_type=pl.DeviceIdType.MESH,
+        )
+    pl.semaphore_wait(barrier, row_count + col_count - 2)
+
+    def share_copy(q, step):
+        to_row = (row + step) % row_count
+        return remote(
+            factors_ref.at[to_row, q],
+            b_all.at[q, row, col],
+            share_send.at[q, step - 1],
+            share_recv.at[q, step - 1],
+            {"row": to_row},
+        )
+
+    def share_arrival(q, step):
+        from_row = (row + row_count - step) % row_count
+        here = b_all.at[q, from_row, col]
+        return remote(here, here, share_send.at[q, step - 1], share_recv.at[q, step - 1], {"row": from_row})
+
+    def tile_copy(step):
+        to_col = (col + step) % col_count
+        return remote(
+            tm_ref.at[to_col],
+            t_all.at[row, :, :, col],
+            tile_send.at[step - 1],
+            tile_recv.at[step - 1],
+            {"col": to_col},
+        )
+
+    def tile_arrival(step):
+        from_col = (col + col_count - step) % col_count
+        here = t_all.at[row, :, :, from_col]
+        return remote(here, here, tile_send.at[step - 1], tile_recv.at[step - 1], {"col": from_col})
+
+    def slab_copy(kind):
+        slab = t_all.at[(row, row, across)[kind]]
+        to_row = (sibling, across, sibling)[kind]
+        return remote(slab, slab, slab_send.at[kind], slab_recv.at[kind], {"row": to_row})
+
+    def slab_arrival(kind):
+        slab = t_all.at[(sibling, across, (sibling + 2) % row_count)[kind]]
+        return remote(slab, slab, slab_send.at[kind], slab_recv.at[kind], {"row": sibling})
+
+    def hops(q, way):
+        return col_count // 2 - (q + way) % 2
+
+    def ring_block(q, half, position):
+        return b_all.at[q, pl.ds(half * half_rows, half_rows), ring_column(position, col_count)]
+
+    def ring_copy(way, q, half, hop):
+        sign = 1 - 2 * way
+        block = ring_block(q, half, place - sign * hop)
+        to_col = ring_column(place + sign, col_count)
+        sems = ring_send.at[way, q, half, hop], ring_recv.at[way, q, half, hop]
+        return remote(block, block, *sems, {"col": to_col})
+
+    def ring_arrival(way, q, half, hop):
+        sign = 1 - 2 * way
+        block = ring_block(q, half, place - sign * (hop + 1))
+        to_col = ring_column(place + sign, col_count)
+        sems = ring_send.at[way, q, half, hop], ring_recv.at[way, q, half, hop]
+        return remote(block, block, *sems, {"col": to_col})
+
+    def ring_begin(q):
+        for step in range(1, row_count):
+            share_arrival(q, step).wait_recv()
+        near_share[q].wait()
+        for half in range(2):
+            for way in range(2):
+                ring_copy(way, q, half, 0).start()
+
+    def ring_step(q, hop):
+        for half in range(2):
+            for way in range(2):
+                if hop < hops(q, way):
+                    ring_arrival(way, q, half, hop).wait_recv()
+                    if hop + 1 < hops(q, way):
+                        ring_copy(way, q, half, hop + 1).start()
+
+    near_share = [
+        pltpu.make_async_copy(factors_ref.at[row, q], b_all.at[q, row, col], near_sem.at[q])
         for q in range(q_count)
     ]
-    t_copies = [
-        pltpu.make_async_copy(
-            t_ref.at[r, c, p],
-            t_all.at[p, :, c, :, pl.ds(r * a_local, a_local)],
-            t_sem.at[r, c, p],
-        )
-        for p in range(slots)
-        for c in range(col_count)
-        for r in range(row_count)
-    ]
-    for copy in b_copies[0] + t_copies:
-        copy.start()
-    for some in b_copies[1:]:
-        for copy in some:
-            copy.start()
-    if last:
-        prior_copy = pltpu.make_async_copy(prior_ref, total, p_sem)
-        prior_copy.start()
-    for copy in t_copies:
-        copy.wait()
-
+    near_tile = pltpu.make_async_copy(
+        tm_ref.at[col], t_all.at[row, :, :, col], near_sem.at[q_count]
+    )
     for q in range(q_count):
-        for copy in b_copies[q]:
-            copy.wait()
-        if q == 0 and last:
-            prior_copy.wait()
+        near_share[q].start()
+        for step in range(1, row_count):
+            share_copy(q, step).start()
+    near_tile.start()
+    for step in range(1, col_count):
+        tile_copy(step).start()
+
+    block = 512
+    blocks = virt // block
+    rows_per = block // a_local
+    ring_hops = col_count // 2
+
+    ring_begin(0)
+    ring_begin(1)
+    ring_step(0, 0)
+    for step in range(1, col_count):
+        tile_arrival(step).wait_recv()
+    near_tile.wait()
+    slab_copy(0).start()
+    slab_copy(1).start()
+    for hop in range(1, ring_hops - 1):
+        ring_step(0, hop)
+    slab_arrival(1).wait_recv()
+    slab_copy(2).start()
+    ring_step(0, ring_hops - 1)
+    slab_arrival(0).wait_recv()
+    slab_arrival(2).wait_recv()
+
+    for q in range(q_count):
+        if q + 2 < q_count:
+            ring_begin(q + 2)
+        hop_done = 0
         for p in range(slots):
 
-            @pl.loop(0, blocks * blocks)
+            @pl.loop(0, blocks * row_count)
             def _(step):
-                m, n = step // blocks, step % blocks
+                m, n = step // row_count, step % row_count
                 left = b_all[q, pl.ds(m * rows_per, rows_per)].reshape(block, virt)
-                cols = pl.ds(pl.multiple_of(n * block, block), block)
-                right = t_all[p, :, :, :, cols].reshape(virt, block)
-                inner[pl.ds(pl.multiple_of(m * block, block), block), cols] = jnp.dot(
-                    left, right, preferred_element_type=jnp.float32
-                ).astype(jnp.bfloat16)
+                right = t_all[n, p].reshape(virt, a_local)
+                inner[
+                    pl.ds(pl.multiple_of(m * block, block), block),
+                    pl.ds(pl.multiple_of(n * a_local, a_local), a_local),
+                ] = jnp.dot(left, right, preferred_element_type=jnp.float32).astype(jnp.bfloat16)
+
+            if q + 1 < q_count and hop_done < ring_hops:
+                ring_step(q + 1, hop_done)
+                hop_done += 1
 
             @pl.loop(0, blocks * blocks)
             def _(step):
@@ -121,15 +252,34 @@
                     (((1,), (1,)), ((), ())),
                     preferred_element_type=jnp.float32,
                 )
-                if q > 0 or last:
+                if q > 0:
                     part = part + total[p, some, cols]
-                if last and q == q_count - 1:
+                if q == q_count - 1:
                     for k in range(rows_per):
                         out_ref[n * rows_per + k, p, some, :] = part[
                             :, k * a_local : (k + 1) * a_local
                         ].astype(jnp.bfloat16)
                 else:
                     total[p, some, cols] = part
+
+            if q + 1 < q_count and hop_done < ring_hops:
+                ring_step(q + 1, hop_done)
+                hop_done += 1
+        if q + 1 < q_count:
+            for hop in range(hop_done, ring_hops):
+                ring_step(q + 1, hop)
+
+    for q in range(q_count):
+        for step in range(1, row_count):
+            share_copy(q, step).wait_send()
+        for half in range(2):
+            for way in range(2):
+                for hop in range(hops(q, way)):
+                    ring_copy(way, q, half, hop).wait_send()
+    for step in range(1, col_count):
+        tile_copy(step).wait_send()
+    for kind in range(3):
+        slab_copy(kind).wait_send()
 
 
 def resid_kernel(ladder_ref, s_ref, resid_ref, swap_ref):
@@ -213,14 +363,6 @@
         vir_energy.reshape(row_count, col_count, group), col_id, 1, 1
     ).reshape(1, b_local)
 
-    chunks = 2
-    per_chunk = share // chunks
-    by_share = factors.reshape(row_count, chunks, per_chunk, group, virt)
-    gathered = []
-    for k in range(chunks):
-        rows_of = lax.all_to_all(by_share[:, k], "row", split_axis=0, concat_axis=0, tiled=True)
-        gathered.append(lax.all_gather(rows_of, "col", axis=0))
-
     block = (col_count, slots, row_count, group, a_local)
     tm_blocks, s_blocks = pl.pallas_call(
         functools.partial(pack_kernel, table),
@@ -231,42 +373,39 @@
         compiler_params=params(),
         name="pack_tiles",
     )(amps, source, mask)
-    tm_mine = lax.all_to_all(tm_blocks, "col", split_axis=0, concat_axis=0, tiled=True)
+    sem = pltpu.SemaphoreType.DMA
+    ring_sems = sem((2, share, 2, col_count // 2))
+    partial = pl.pallas_call(
+        ladder_kernel,
+        out_shape=jax.ShapeDtypeStruct((row_count, slots, virt, a_local), bf16),
+        in_specs=[pl.BlockSpec(memory_space=VMEM), pl.BlockSpec(memory_space=pl.ANY)],
+        out_specs=pl.BlockSpec(memory_space=VMEM),
+        scratch_shapes=[
+            VMEM((row_count, slots, row_count, col_count, group, a_local), bf16),
+            VMEM((share, row_count, col_count, group, virt), bf16),
+            VMEM((virt, virt), bf16),
+            VMEM((slots, virt, virt), f32),
+            sem((share + 1,)),
+            sem((share, row_count - 1)),
+            sem((share, row_count - 1)),
+            sem((col_count - 1,)),
+            sem((col_count - 1,)),
+            sem((3,)),
+            sem((3,)),
+            ring_sems,
+            ring_sems,
+        ],
+        compiler_params=pltpu.CompilerParams(
+            vmem_limit_bytes=56 * 1024 * 1024, collective_id=0, has_side_effects=True
+        ),
+        cost_estimate=pl.CostEstimate(
+            flops=4 * share * slots * virt**3, bytes_accessed=16 * 1024 * 1024, transcendentals=0
+        ),
+        name="ladder",
+    )(tm_blocks, factors.reshape(row_count, share, group, virt))
     s_mine = lax.all_to_all(s_blocks, "col", split_axis=0, concat_axis=0, tiled=True)
-    tm_all = lax.all_gather(tm_mine, "row", axis=0)
-
-    flops = 4 * per_chunk * slots * virt**3
-    prior = None
-    for k in range(chunks):
-        last = k == chunks - 1
-        operands = [tm_all, gathered[k]] + ([prior] if last else [])
-        total = (slots, virt, virt)
-        prior = pl.pallas_call(
-            functools.partial(ladder_kernel, last),
-            out_shape=(
-                jax.ShapeDtypeStruct((row_count, slots, virt, a_local), bf16)
-                if last
-                else jax.ShapeDtypeStruct(total, f32)
-            ),
-            in_specs=[pl.BlockSpec(memory_space=pl.ANY)] * len(operands),
-            out_specs=pl.BlockSpec(memory_space=VMEM),
-            scratch_shapes=([VMEM(total, f32)] if last else [])
-            + [
-                VMEM((slots, row_count, col_count, group, virt), bf16),
-                VMEM((per_chunk, row_count, col_count, group, virt), bf16),
-                VMEM((virt, virt), bf16),
-                pltpu.SemaphoreType.DMA((row_count, col_count, slots)),
-                pltpu.SemaphoreType.DMA((per_chunk, col_count)),
-            ]
-            + ([pltpu.SemaphoreType.DMA] if last else []),
-            compiler_params=params(),
-            cost_estimate=pl.CostEstimate(
-                flops=flops, bytes_accessed=16 * 1024 * 1024, transcendentals=0
-            ),
-            name="ladder_end" if last else "ladder_begin",
-        )(*operands)
-
-    ladder = lax.psum_scatter(prior, "row", scatter_dimension=0, tiled=True)
+
+    ladder = lax.psum_scatter(partial, "row", scatter_dimension=0, tiled=True)
     ladder = ladder.reshape(slots, virt, a_local)
     resid, swap = pl.pallas_call(
         resid_kernel,
@@ -402,7 +541,9 @@
         and occ_count % 2 == 0
         and 2 * col_count == occ_count * occ_count
         and amps.shape[2] == occ_count * occ_count
-        and aux_count % (2 * row_count) == 0
+        and aux_count % row_count == 0
+        and aux_count >= 2 * row_count
+        and row_count == 4
         and virt % 512 == 0
         and 512 % a_local == 0
     )

time: 367 us -> 276 us (0.75)
  waiting for transfers between devices: 144 us -> 36.9 us
  Pallas kernels: 80 us -> 168 us
  blocking collectives: 117 us -> 46.2 us
    all_gather x3 -> x0, waiting for transfers between devices: 108 us -> none  [the longest x2 73.3 us: fast_shards(): gathered.append(lax.all_gather(rows_of, 'col', axis=0))]
    pallas_call x2 -> x1, Pallas kernels: 62 us -> 150 us  [fast_shards(): pl.pallas_call(ladder_kernel, out_shape=jax.ShapeDtypeStruct((row_count,...]
    all_to_all x3 -> x0, blocking collectives: 69.6 us -> none  [the longest x1 44.7 us: fast_shards(): lax.all_to_all(tm_blocks, 'col', split_axis=0, concat_axis=0, tiled=True)]
  transfers between devices with their start and end apart: 5 -> 2, of which waited for: 5 -> 2; matrix products, arithmetic and copies ran while one was open for 1% -> 1% of each run, Pallas kernels for 10% -> 0%
where the time goes in v2:
time: 276 us
  Pallas kernels  168 us (61%)
  blocking collectives  46.2 us (17%)
  waiting for transfers between devices  36.9 us (13%)
  between operations  13.4 us (5%)
  local copies, waits for them, and re-layouts  5.84 us (2%)
  starting transfers between devices  5.53 us (2%)
    pallas_call x1, Pallas kernels, fast_shards(): pl.pallas_call(ladder_kernel, out_shape=jax.ShapeDtypeStruct((row_count,...  150 us
    all_to_all x1, blocking collectives, fast_shards(): lax.all_to_all(s_blocks, 'col', split_axis=0, concat_axis=0, tiled=True)  27.3 us
    all_to_all x1, waiting for transfers between devices, fast_shards(): rsym = lax.all_to_all(rsym, 'col', split_axis=0, concat_axis=0, tiled=True)  23.5 us
    all_to_all x1, blocking collectives, fast_shards(): lax.all_to_all(swap, 'row', split_axis=0, concat_axis=0, tiled=True)  18.9 us
    reduce_scatter x1, waiting for transfers between devices, fast_shards(): ladder = lax.psum_scatter(partial, 'row', scatter_dimension=0, tiled=True)  13.4 us
    pallas_call x1, Pallas kernels, fast_shards(): pl.pallas_call(functools.partial(pack_kernel, table), out_shape=[jax.Shap...  6.79 us
    all_to_all x1, starting transfers between devices, fast_shards(): rsym = lax.all_to_all(rsym, 'col', split_axis=0, concat_axis=0, tiled=True)  5.53 us
  transfers between devices with their start and end apart: 2, of which 2 were waited for; matrix products, arithmetic and copies ran while one was open for 1% of the time, Pallas kernels for 0%

profile of v2, /device:TPU:0, one launch (start us, length us, event | category | flops | bytes accessed | tf_op | source)
XLA Modules:
  0.0 275.6 jit_solution(3621362627446823407)
XLA Ops:
  6.5 0.0 copy-start
  6.5 0.0 reduce-scatter.2.cloned.1.call-start
  6.5 0.8 copy-done
  7.3 0.1 copy.9
  7.4 0.1 broadcast_in_dim.10
  7.5 0.7 reshape.55.mask_ref
  8.2 6.8 %pack_tiles.1 = (bf16[8,2,4,32,256]{4,3,2,1,0:T(8,128)(2,1)}, bf16[8,2,4,32,256]{4,3,2,1,0:T(8,128)(2,1)}) custom-call(bf16[16,32768]{1,0:T(8,128)(2,1)} %bitcast.9, bf16[16,32768]{1,0:T(8,128)(2,1)} %bitcast.11, f32[2,16,128]{2,1,0:T(8,128)} %reshape.55.mask_ref), custom_call_target="tpu_custom_call" | custom-call | tf_op jit(solution)/shard_map/pack_tiles/pallas_call | solution.py:367
  15.0 149.7 %ladder.1 = bf16[4,2,1024,256]{3,2,1,0:T(8,128)(2,1)} custom-call(bf16[8,2,4,32,256]{4,3,2,1,0:T(8,128)(2,1)} %get-tuple-element.9.tm_ref, bf16[4,4,32,1024]{3,2,1,0:T(8,128)(2,1)} %bitcast.15), custom_call_target="tpu_custom_call" | custom-call | flops 34359738368 | bytes 16777216 | tf_op jit(solution)/shard_map/ladder/pallas_call | solution.py:378
  164.7 0.0 copy-start.2
  164.7 0.0 reduce-scatter.2.cloned.1.call-update
  164.7 1.2 copy-done.2
  165.9 27.3 %all_to_all.15.s_ref = bf16[8,2,4,32,256]{4,3,2,1,0:T(8,128)(2,1)} all-to-all(bf16[8,2,4,32,256]{4,3,2,1,0:T(8,128)(2,1)S(1)} %copy-done.2), channel_id=1, replica_groups=mesh['row'=4,'col'=8] {'col'}, dimensions={0} | all-to-all | bytes 2097152 | tf_op jit(solution)/shard_map/all_to_all | solution.py:406
  193.2 13.4 %reduce-scatter.2.cloned.1.call-done = bf16[1,2,1024,256]{3,2,1,0:T(8,128)(2,1)} async-done(((bf16[4,2,1024,256]{3,2,1,0:T(8,128)(2,1)}), bf16[1,2,1024,256]{3,2,1,0:T(8,128)(2,1)}) %reduce-scatter.2.cloned.1.call-update) | async-done | bytes 1048592 | tf_op jit(solution)/shard_map/reduce_scatter | solution.py:408
  206.6 3.5 %resid.1 = (f32[2,1024,256]{2,1,0:T(8,128)}, bf16[4,2,256,256]{3,2,1,0:T(8,128)(2,1)}) custom-call(bf16[2,1024,256]{2,1,0:T(8,128)(2,1)} %bitcast.12, bf16[8,2,4,32,256]{4,3,2,1,0:T(8,128)(2,1)} %all_to_all.15.s_ref), custom_call_target="tpu_custom_call" | custom-call | tf_op jit(solution)/shard_map/resid/pallas_call | solution.py:410
  210.1 0.0 copy-start.3
  210.1 0.0 copy-start.4
  210.1 18.9 %all_to_all.16.swap_ref = bf16[4,2,256,256]{3,2,1,0:T(8,128)(2,1)} all-to-all(bf16[4,2,256,256]{3,2,1,0:T(8,128)(2,1)} %get-tuple-element.12), channel_id=1, replica_groups=mesh['row'=4,'col'=8] {'row'}, dimensions={0} | all-to-all | bytes 2097152 | tf_op jit(solution)/shard_map/all_to_all | solution.py:421
  229.0 3.0 %add_swapped.1 = bf16[8,2,4,32,256]{4,3,2,1,0:T(8,128)(2,1)} custom-call(f32[2,1024,256]{2,1,0:T(8,128)} %get-tuple-element.11.resid_ref, bf16[4,2,256,256]{3,2,1,0:T(8,128)(2,1)} %all_to_all.16.swap_ref), custom_call_target="tpu_custom_call" | custom-call | tf_op jit(solution)/shard_map/add_swapped/pallas_call | solution.py:422
  232.0 5.5 %all-to-all-start.2 = ((bf16[8,2,4,32,256]{4,3,2,1,0:T(8,128)(2,1)}), bf16[8,2,4,32,256]{4,3,2,1,0:T(8,128)(2,1)S(1)}, u32[]{:S(2)}, u32[]{:S(2)}) async-start(bf16[8,2,4,32,256]{4,3,2,1,0:T(8,128)(2,1)} %add_swapped.1), calls=%async_computation.3 | async-start | bytes 2097152 | tf_op jit(solution)/shard_map/all_to_all | solution.py:430
  237.6 0.0 copy-done.3
  237.6 0.1 reshape.58
  237.7 0.6 reshape.59.vir_b_ref
  238.3 0.6 dynamic_slice.15.vir_a_ref
  238.9 0.0 copy-done.4
  238.9 0.1 broadcast_add_fusion
  239.0 0.7 add.46.occ_ref
  239.7 23.5 %all-to-all-done.2.rsym_ref = bf16[8,2,4,32,256]{4,3,2,1,0:T(8,128)(2,1)S(1)} async-done(((bf16[8,2,4,32,256]{4,3,2,1,0:T(8,128)(2,1)}), bf16[8,2,4,32,256]{4,3,2,1,0:T(8,128)(2,1)S(1)}, u32[]{:S(2)}, u32[]{:S(2)}) %all-to-all-start.2) | async-done | bytes 1048608 | tf_op jit(solution)/shard_map/all_to_all | solution.py:430
  263.1 0.0 copy-start.1
  263.2 1.0 copy-done.1
  264.1 4.7 %update.1 = bf16[16,32768]{1,0:T(8,128)(2,1)} custom-call(bf16[16,32768]{1,0:T(8,128)(2,1)} %bitcast.10, bf16[8,2,4,32,256]{4,3,2,1,0:T(8,128)(2,1)} %copy-done.1, f32[2,16,128]{2,1,0:T(8,128)} %reshape.55.mask_ref, f32[16,1]{1,0:T(8,128)} %add.46.occ_ref, f32[1,128]{1,0:T(1,128)} %reshape.59.vir_b_ref, f32[256]{0:T(256)} %dynamic_slice.15.vir_a_ref), custom_call_target="tpu_custom_call" | custom-call | tf_op jit(solution)/shard_map/update/pallas_call | solution.py:431
  (3 shorter events, 0.0 us)
Async XLA Ops:
  6.5 0.8 copy-start
  6.5 200.1 %reduce-scatter.2.cloned.1.call-start = ((), (), s32[]{:S(2)}) async-start(), calls=%async_computation.4 | async-start | bytes 5242880 | tf_op jit(solution)/shard_map/reduce_scatter | solution.py:408
  164.7 1.2 copy-start.2
  210.1 27.4 %copy-start.3 = (f32[1024]{0:T(1024)S(1)}, f32[1024]{0:T(1024)}, u32[]{:S(2)}) copy-start(f32[1024]{0:T(1024)} %param.11) | copy-start | bytes 12292
  210.1 28.8 %copy-start.4 = (f32[4]{0:T(128)S(1)}, f32[4]{0:T(128)}, u32[]{:S(2)}) copy-start(f32[4]{0:T(128)} %param.10) | copy-start | bytes 52
  232.0 31.1 %all-to-all-start.2 = ((bf16[8,2,4,32,256]{4,3,2,1,0:T(8,128)(2,1)}), bf16[8,2,4,32,256]{4,3,2,1,0:T(8,128)(2,1)S(1)}, u32[]{:S(2)}, u32[]{:S(2)}) async-start(bf16[8,2,4,32,256]{4,3,2,1,0:T(8,128)(2,1)} %add_swapped.1), calls=%async_computation.3 | async-start | bytes 2097152 | tf_op jit(solution)/shard_map/all_to_all | solution.py:430
  263.1 1.0 copy-start.1
Sparse Core Ops, SparseCore 0:
  164.9 41.6 reduce-scatter.1

commit v3 on v2

--- a/solution.py
+++ b/solution.py
@@ -202,28 +202,34 @@
     block = 512
     blocks = virt // block
     rows_per = block // a_local
-    ring_hops = col_count // 2
+    stagger = col_count // 4
+
+    def ring_slot(slot):
+        q = slot // stagger
+        if (slot + 1) % stagger == 0 and q + 1 < q_count:
+            ring_begin(q + 1)
+        if q < q_count:
+            ring_step(q, slot % stagger)
+        if q > 0:
+            ring_step(q - 1, stagger + slot % stagger)
 
     ring_begin(0)
-    ring_begin(1)
-    ring_step(0, 0)
+    ring_slot(0)
     for step in range(1, col_count):
         tile_arrival(step).wait_recv()
     near_tile.wait()
     slab_copy(0).start()
     slab_copy(1).start()
-    for hop in range(1, ring_hops - 1):
-        ring_step(0, hop)
+    for slot in range(1, stagger):
+        ring_slot(slot)
     slab_arrival(1).wait_recv()
     slab_copy(2).start()
-    ring_step(0, ring_hops - 1)
+    for slot in range(stagger, 2 * stagger):
+        ring_slot(slot)
     slab_arrival(0).wait_recv()
     slab_arrival(2).wait_recv()
 
     for q in range(q_count):
-        if q + 2 < q_count:
-            ring_begin(q + 2)
-        hop_done = 0
         for p in range(slots):
 
             @pl.loop(0, blocks * row_count)
@@ -235,10 +241,6 @@
                     pl.ds(pl.multiple_of(m * block, block), block),
                     pl.ds(pl.multiple_of(n * a_local, a_local), a_local),
                 ] = jnp.dot(left, right, preferred_element_type=jnp.float32).astype(jnp.bfloat16)
-
-            if q + 1 < q_count and hop_done < ring_hops:
-                ring_step(q + 1, hop_done)
-                hop_done += 1
 
             @pl.loop(0, blocks * blocks)
             def _(step):
@@ -262,12 +264,9 @@
                 else:
                     total[p, some, cols] = part
 
-            if q + 1 < q_count and hop_done < ring_hops:
-                ring_step(q + 1, hop_done)
-                hop_done += 1
-        if q + 1 < q_count:
-            for hop in range(hop_done, ring_hops):
-                ring_step(q + 1, hop)
+            if q + 1 < q_count:
+                for slot in range(p * stagger // slots, (p + 1) * stagger // slots):
+                    ring_slot((q + 2) * stagger + slot)
 
     for q in range(q_count):
         for step in range(1, row_count):
@@ -544,6 +543,7 @@
         and aux_count % row_count == 0
         and aux_count >= 2 * row_count
         and row_count == 4
+        and col_count % 4 == 0
         and virt % 512 == 0
         and 512 % a_local == 0
     )

time: 276 us -> 274 us (level)
  Pallas kernels: 168 us -> 161 us
  waiting for transfers between devices: 36.9 us -> 41.6 us
    pallas_call x1, Pallas kernels: 150 us -> 143 us  [fast_shards(): pl.pallas_call(ladder_kernel, out_shape=jax.ShapeDtypeStruct((row_count,...]
    reduce_scatter x1, waiting for transfers between devices: 13.4 us -> 18.1 us  [fast_shards(): ladder = lax.psum_scatter(partial, 'row', scatter_dimension=0, tiled=True)]
where the time goes in v3:
time: 274 us; the launch traced here: 273 us
  Pallas kernels  161 us (59%)
  blocking collectives  45.2 us (16%)
  waiting for transfers between devices  41.6 us (15%)
  between operations  13.4 us (5%)
  local copies, waits for them, and re-layouts  5.84 us (2%)
  starting transfers between devices  5.53 us (2%)
    pallas_call x1, Pallas kernels, fast_shards(): pl.pallas_call(ladder_kernel, out_shape=jax.ShapeDtypeStruct((row_count,...  143 us
    all_to_all x1, blocking collectives, fast_shards(): lax.all_to_all(s_blocks, 'col', split_axis=0, concat_axis=0, tiled=True)  26.3 us
    all_to_all x1, waiting for transfers between devices, fast_shards(): rsym = lax.all_to_all(rsym, 'col', split_axis=0, concat_axis=0, tiled=True)  23.5 us
    all_to_all x1, blocking collectives, fast_shards(): lax.all_to_all(swap, 'row', split_axis=0, concat_axis=0, tiled=True)  18.9 us
    reduce_scatter x1, waiting for transfers between devices, fast_shards(): ladder = lax.psum_scatter(partial, 'row', scatter_dimension=0, tiled=True)  18.1 us
    pallas_call x1, Pallas kernels, fast_shards(): pl.pallas_call(functools.partial(pack_kernel, table), out_shape=[jax.Shap...  6.79 us
    all_to_all x1, starting transfers between devices, fast_shards(): rsym = lax.all_to_all(rsym, 'col', split_axis=0, concat_axis=0, tiled=True)  5.53 us
  transfers between devices with their start and end apart: 2, of which 2 were waited for; matrix products, arithmetic and copies ran while one was open for 1% of the time, Pallas kernels for 0%

profile of v3, /device:TPU:0, one launch (start us, length us, event | category | flops | bytes accessed | tf_op | source)
XLA Modules:
  0.0 273.0 jit_solution(17224130795564309477)
XLA Ops:
  6.5 0.0 copy-start
  6.5 0.0 reduce-scatter.2.cloned.1.call-start
  6.5 0.8 copy-done
  7.3 0.1 copy.9
  7.4 0.1 broadcast_in_dim.10
  7.5 0.7 reshape.55.mask_ref
  8.2 6.8 %pack_tiles.1 = (bf16[8,2,4,32,256]{4,3,2,1,0:T(8,128)(2,1)}, bf16[8,2,4,32,256]{4,3,2,1,0:T(8,128)(2,1)}) custom-call(bf16[16,32768]{1,0:T(8,128)(2,1)} %bitcast.9, bf16[16,32768]{1,0:T(8,128)(2,1)} %bitcast.11, f32[2,16,128]{2,1,0:T(8,128)} %reshape.55.mask_ref), custom_call_target="tpu_custom_call" | custom-call | tf_op jit(solution)/shard_map/pack_tiles/pallas_call | solution.py:366
  15.0 143.3 %ladder.1 = bf16[4,2,1024,256]{3,2,1,0:T(8,128)(2,1)} custom-call(bf16[8,2,4,32,256]{4,3,2,1,0:T(8,128)(2,1)} %get-tuple-element.9.tm_ref, bf16[4,4,32,1024]{3,2,1,0:T(8,128)(2,1)} %bitcast.15), custom_call_target="tpu_custom_call" | custom-call | flops 34359738368 | bytes 16777216 | tf_op jit(solution)/shard_map/ladder/pallas_call | solution.py:377
  158.3 0.0 copy-start.2
  158.3 0.0 reduce-scatter.2.cloned.1.call-update
  158.3 1.2 copy-done.2
  159.5 26.3 %all_to_all.15.s_ref = bf16[8,2,4,32,256]{4,3,2,1,0:T(8,128)(2,1)} all-to-all(bf16[8,2,4,32,256]{4,3,2,1,0:T(8,128)(2,1)S(1)} %copy-done.2), channel_id=1, replica_groups=mesh['row'=4,'col'=8] {'col'}, dimensions={0} | all-to-all | bytes 2097152 | tf_op jit(solution)/shard_map/all_to_all | solution.py:405
  185.8 18.1 %reduce-scatter.2.cloned.1.call-done = bf16[1,2,1024,256]{3,2,1,0:T(8,128)(2,1)} async-done(((bf16[4,2,1024,256]{3,2,1,0:T(8,128)(2,1)}), bf16[1,2,1024,256]{3,2,1,0:T(8,128)(2,1)}) %reduce-scatter.2.cloned.1.call-update) | async-done | bytes 1048592 | tf_op jit(solution)/shard_map/reduce_scatter | solution.py:407
  203.9 3.5 %resid.1 = (f32[2,1024,256]{2,1,0:T(8,128)}, bf16[4,2,256,256]{3,2,1,0:T(8,128)(2,1)}) custom-call(bf16[2,1024,256]{2,1,0:T(8,128)(2,1)} %bitcast.12, bf16[8,2,4,32,256]{4,3,2,1,0:T(8,128)(2,1)} %all_to_all.15.s_ref), custom_call_target="tpu_custom_call" | custom-call | tf_op jit(solution)/shard_map/resid/pallas_call | solution.py:409
  207.5 0.0 copy-start.3
  207.5 0.0 copy-start.4
  207.5 18.9 %all_to_all.16.swap_ref = bf16[4,2,256,256]{3,2,1,0:T(8,128)(2,1)} all-to-all(bf16[4,2,256,256]{3,2,1,0:T(8,128)(2,1)} %get-tuple-element.12), channel_id=1, replica_groups=mesh['row'=4,'col'=8] {'row'}, dimensions={0} | all-to-all | bytes 2097152 | tf_op jit(solution)/shard_map/all_to_all | solution.py:420
  226.4 3.0 %add_swapped.1 = bf16[8,2,4,32,256]{4,3,2,1,0:T(8,128)(2,1)} custom-call(f32[2,1024,256]{2,1,0:T(8,128)} %get-tuple-element.11.resid_ref, bf16[4,2,256,256]{3,2,1,0:T(8,128)(2,1)} %all_to_all.16.swap_ref), custom_call_target="tpu_custom_call" | custom-call | tf_op jit(solution)/shard_map/add_swapped/pallas_call | solution.py:421
  229.4 5.5 %all-to-all-start.2 = ((bf16[8,2,4,32,256]{4,3,2,1,0:T(8,128)(2,1)}), bf16[8,2,4,32,256]{4,3,2,1,0:T(8,128)(2,1)S(1)}, u32[]{:S(2)}, u32[]{:S(2)}) async-start(bf16[8,2,4,32,256]{4,3,2,1,0:T(8,128)(2,1)} %add_swapped.1), calls=%async_computation.3 | async-start | bytes 2097152 | tf_op jit(solution)/shard_map/all_to_all | solution.py:429
  234.9 0.0 copy-done.3
  234.9 0.1 reshape.58
  235.0 0.6 reshape.59.vir_b_ref
  235.6 0.6 dynamic_slice.15.vir_a_ref
  236.2 0.0 copy-done.4
  236.2 0.1 broadcast_add_fusion
  236.3 0.7 add.46.occ_ref
  237.0 23.5 %all-to-all-done.2.rsym_ref = bf16[8,2,4,32,256]{4,3,2,1,0:T(8,128)(2,1)S(1)} async-done(((bf16[8,2,4,32,256]{4,3,2,1,0:T(8,128)(2,1)}), bf16[8,2,4,32,256]{4,3,2,1,0:T(8,128)(2,1)S(1)}, u32[]{:S(2)}, u32[]{:S(2)}) %all-to-all-start.2) | async-done | bytes 1048608 | tf_op jit(solution)/shard_map/all_to_all | solution.py:429
  260.5 0.0 copy-start.1
  260.5 1.0 copy-done.1
  261.4 4.7 %update.1 = bf16[16,32768]{1,0:T(8,128)(2,1)} custom-call(bf16[16,32768]{1,0:T(8,128)(2,1)} %bitcast.10, bf16[8,2,4,32,256]{4,3,2,1,0:T(8,128)(2,1)} %copy-done.1, f32[2,16,128]{2,1,0:T(8,128)} %reshape.55.mask_ref, f32[16,1]{1,0:T(8,128)} %add.46.occ_ref, f32[1,128]{1,0:T(1,128)} %reshape.59.vir_b_ref, f32[256]{0:T(256)} %dynamic_slice.15.vir_a_ref), custom_call_target="tpu_custom_call" | custom-call | tf_op jit(solution)/shard_map/update/pallas_call | solution.py:430
  (3 shorter events, 0.0 us)
Async XLA Ops:
  6.5 0.8 copy-start
  6.5 197.4 %reduce-scatter.2.cloned.1.call-start = ((), (), s32[]{:S(2)}) async-start(), calls=%async_computation.4 | async-start | bytes 5242880 | tf_op jit(solution)/shard_map/reduce_scatter | solution.py:407
  158.3 1.2 copy-start.2
  207.5 27.4 %copy-start.3 = (f32[1024]{0:T(1024)S(1)}, f32[1024]{0:T(1024)}, u32[]{:S(2)}) copy-start(f32[1024]{0:T(1024)} %param.11) | copy-start | bytes 12292
  207.5 28.8 %copy-start.4 = (f32[4]{0:T(128)S(1)}, f32[4]{0:T(128)}, u32[]{:S(2)}) copy-start(f32[4]{0:T(128)} %param.10) | copy-start | bytes 52
  229.4 31.1 %all-to-all-start.2 = ((bf16[8,2,4,32,256]{4,3,2,1,0:T(8,128)(2,1)}), bf16[8,2,4,32,256]{4,3,2,1,0:T(8,128)(2,1)S(1)}, u32[]{:S(2)}, u32[]{:S(2)}) async-start(bf16[8,2,4,32,256]{4,3,2,1,0:T(8,128)(2,1)} %add_swapped.1), calls=%async_computation.3 | async-start | bytes 2097152 | tf_op jit(solution)/shard_map/all_to_all | solution.py:429
  260.5 1.0 copy-start.1
Sparse Core Ops, SparseCore 0:
  158.4 45.4 reduce-scatter.1

commit v4 on v3

--- a/solution.py
+++ b/solution.py
@@ -57,13 +57,23 @@
 
 
 def ladder_kernel(
+    diagonal_from,
     tm_ref,
+    s_ref,
     factors_ref,
     out_ref,
     t_all,
     b_all,
     inner,
     total,
+    part,
+    core_in,
+    across_in,
+    s_all,
+    resid,
+    swap_out,
+    swap_in,
+    rsym,
     near_sem,
     share_send,
     share_recv,
@@ -73,12 +83,25 @@
     slab_recv,
     ring_send,
     ring_recv,
+    s_send,
+    s_recv,
+    core_send,
+    core_recv,
+    across_send,
+    across_recv,
+    swap_send,
+    swap_recv,
+    back_send,
+    back_recv,
 ):
     q_count, row_count, col_count, group, virt = b_all.shape
     slots, a_local = t_all.shape[1], t_all.shape[5]
     row, col = lax.axis_index("row"), lax.axis_index("col")
     sibling = row + 1 - 2 * (row % 2)
     across = (row + 2) % row_count
+    diagonal = (sibling + 2) % row_count
+    chip = row // 2
+    rows_by = (row, sibling, across, diagonal)
     place = (col // 2) * (1 - col % 2) + (col_count - 1 - col // 2) * (col % 2)
     half_rows = row_count // 2
 
@@ -139,14 +162,18 @@
         here = t_all.at[row, :, :, from_col]
         return remote(here, here, tile_send.at[step - 1], tile_recv.at[step - 1], {"col": from_col})
 
-    def slab_copy(kind):
-        slab = t_all.at[(row, row, across)[kind]]
+    def slab_copy(kind, step):
+        from_col = (col + col_count - step) % col_count
+        slab = t_all.at[(row, row, across)[kind], :, :, from_col]
         to_row = (sibling, across, sibling)[kind]
-        return remote(slab, slab, slab_send.at[kind], slab_recv.at[kind], {"row": to_row})
-
-    def slab_arrival(kind):
-        slab = t_all.at[(sibling, across, (sibling + 2) % row_count)[kind]]
-        return remote(slab, slab, slab_send.at[kind], slab_recv.at[kind], {"row": sibling})
+        sems = slab_send.at[kind, step], slab_recv.at[kind, step]
+        return remote(slab, slab, *sems, {"row": to_row})
+
+    def slab_arrival(kind, step):
+        from_col = (col + col_count - step) % col_count
+        slab = t_all.at[(sibling, across, diagonal)[kind], :, :, from_col]
+        sems = slab_send.at[kind, step], slab_recv.at[kind, step]
+        return remote(slab, slab, *sems, {"row": sibling})
 
     def hops(q, way):
         return col_count // 2 - (q + way) % 2
@@ -184,6 +211,68 @@
                     if hop + 1 < hops(q, way):
                         ring_copy(way, q, half, hop + 1).start()
 
+    def s_copy(step):
+        to_col = (col + step) % col_count
+        sems = s_send.at[step - 1], s_recv.at[step - 1]
+        return remote(s_ref.at[to_col], s_all.at[col], *sems, {"col": to_col})
+
+    def s_arrival(step):
+        from_col = (col + col_count - step) % col_count
+        here = s_all.at[from_col]
+        return remote(here, here, s_send.at[step - 1], s_recv.at[step - 1], {"col": from_col})
+
+    def core_copy(p, near):
+        source = part.at[sibling if near else diagonal, p]
+        dest = core_in.at[chip if near else 1 - chip, p]
+        return remote(source, dest, core_send.at[p, near], core_recv.at[p, near], {"row": sibling})
+
+    def core_arrival(p, near):
+        here = core_in.at[chip if near else 1 - chip, p]
+        return remote(here, here, core_send.at[p, near], core_recv.at[p, near], {"row": sibling})
+
+    def across_copy(p):
+        sems = across_send.at[p], across_recv.at[p]
+        return remote(part.at[across, p], across_in.at[p], *sems, {"row": across})
+
+    def across_arrival(p):
+        here = across_in.at[p]
+        return remote(here, here, across_send.at[p], across_recv.at[p], {"row": across})
+
+    def send_across(p):
+        core_arrival(p, 0).wait_recv()
+
+        @pl.loop(0, row_count)
+        def _(y):
+            some = pl.ds(pl.multiple_of(y * a_local, a_local), a_local)
+            both = part[across, p, some, :].astype(jnp.float32) + core_in[
+                1 - chip, p, some, :
+            ].astype(jnp.float32)
+            part[across, p, some, :] = both.astype(jnp.bfloat16)
+
+        across_copy(p).start()
+
+    def swap_copy(kind, p):
+        sems = swap_send.at[kind - 1, p], swap_recv.at[kind - 1, p]
+        return remote(swap_out.at[kind - 1, p], swap_in.at[row, p], *sems, {"row": rows_by[kind]})
+
+    def swap_arrival(kind, p):
+        here = swap_in.at[rows_by[kind], p]
+        sems = swap_send.at[kind - 1, p], swap_recv.at[kind - 1, p]
+        return remote(here, here, *sems, {"row": rows_by[kind]})
+
+    def back_copy(kind, step):
+        to_col = (col + step) % col_count
+        sems = back_send.at[kind, step - 1], back_recv.at[kind, step - 1]
+        dest = out_ref.at[col, rows_by[kind]]
+        return remote(rsym.at[kind, to_col], dest, *sems, {"col": to_col})
+
+    def back_arrival(kind, step):
+        from_col = (col + col_count - step) % col_count
+        here = out_ref.at[from_col, rows_by[kind]]
+        sems = back_send.at[kind, step - 1], back_recv.at[kind, step - 1]
+        return remote(here, here, *sems, {"col": from_col})
+
+    near_s = pltpu.make_async_copy(s_ref.at[col], s_all.at[col], near_sem.at[q_count + 1])
     near_share = [
         pltpu.make_async_copy(factors_ref.at[row, q], b_all.at[q, row, col], near_sem.at[q])
         for q in range(q_count)
@@ -191,13 +280,13 @@
     near_tile = pltpu.make_async_copy(
         tm_ref.at[col], t_all.at[row, :, :, col], near_sem.at[q_count]
     )
+    near_tile.start()
+    for step in range(1, col_count):
+        tile_copy(step).start()
     for q in range(q_count):
         near_share[q].start()
         for step in range(1, row_count):
             share_copy(q, step).start()
-    near_tile.start()
-    for step in range(1, col_count):
-        tile_copy(step).start()
 
     block = 512
     blocks = virt // block
@@ -213,23 +302,30 @@
         if q > 0:
             ring_step(q - 1, stagger + slot % stagger)
 
+    near_tile.wait()
+    slab_copy(0, 0).start()
+    slab_copy(1, 0).start()
     ring_begin(0)
-    ring_slot(0)
     for step in range(1, col_count):
         tile_arrival(step).wait_recv()
-    near_tile.wait()
-    slab_copy(0).start()
-    slab_copy(1).start()
-    for slot in range(1, stagger):
+        slab_copy(0, step).start()
+        slab_copy(1, step).start()
+    for slot in range(stagger):
         ring_slot(slot)
-    slab_arrival(1).wait_recv()
-    slab_copy(2).start()
+    for step in range(col_count):
+        slab_arrival(1, step).wait_recv()
+        slab_copy(2, step).start()
     for slot in range(stagger, 2 * stagger):
         ring_slot(slot)
-    slab_arrival(0).wait_recv()
-    slab_arrival(2).wait_recv()
+    for step in range(col_count):
+        slab_arrival(0, step).wait_recv()
+        slab_arrival(2, step).wait_recv()
 
     for q in range(q_count):
+        if q == q_count - 1:
+            near_s.start()
+            for step in range(1, col_count):
+                s_copy(step).start()
         for p in range(slots):
 
             @pl.loop(0, blocks * row_count)
@@ -242,31 +338,83 @@
                     pl.ds(pl.multiple_of(n * a_local, a_local), a_local),
                 ] = jnp.dot(left, right, preferred_element_type=jnp.float32).astype(jnp.bfloat16)
 
+            if q == q_count - 1 and p > 0:
+                send_across(p - 1)
+
             @pl.loop(0, blocks * blocks)
             def _(step):
                 m, n = step // blocks, step % blocks
                 some = pl.ds(pl.multiple_of(m * block, block), block)
                 cols = pl.ds(pl.multiple_of(n * block, block), block)
                 right = b_all[q, pl.ds(n * rows_per, rows_per)].reshape(block, virt)
-                part = lax.dot_general(
+                product = lax.dot_general(
                     inner[some, :],
                     right,
                     (((1,), (1,)), ((), ())),
                     preferred_element_type=jnp.float32,
                 )
                 if q > 0:
-                    part = part + total[p, some, cols]
+                    product = product + total[p, some, cols]
                 if q == q_count - 1:
                     for k in range(rows_per):
-                        out_ref[n * rows_per + k, p, some, :] = part[
+                        part[n * rows_per + k, p, some, :] = product[
                             :, k * a_local : (k + 1) * a_local
                         ].astype(jnp.bfloat16)
                 else:
-                    total[p, some, cols] = part
+                    total[p, some, cols] = product
 
             if q + 1 < q_count:
                 for slot in range(p * stagger // slots, (p + 1) * stagger // slots):
                     ring_slot((q + 2) * stagger + slot)
+            else:
+                core_copy(p, 0).start()
+                core_copy(p, 1).start()
+
+    send_across(slots - 1)
+    near_s.wait()
+    for step in range(1, col_count):
+        s_arrival(step).wait_recv()
+
+    for p in range(slots):
+        core_arrival(p, 1).wait_recv()
+        across_arrival(p).wait_recv()
+        for y in range(row_count):
+            for c in range(col_count):
+                some = pl.ds(y * a_local + c * group, group)
+                resid[p, some, :] = (
+                    part[row, p, some, :].astype(jnp.float32)
+                    + core_in[chip, p, some, :].astype(jnp.float32)
+                    + across_in[p, some, :].astype(jnp.float32)
+                    + s_all[c, p, y].astype(jnp.float32)
+                )
+        for kind in range(row_count - 1, -1, -1):
+            some = pl.ds(pl.multiple_of(rows_by[kind] * a_local, a_local), a_local)
+            turned = resid[p, some, :].T.astype(jnp.bfloat16)
+            if kind == 0:
+                swap_in[row, p] = turned
+            else:
+                swap_out[kind - 1, p] = turned
+                swap_copy(kind, p).start()
+
+    flip = 1 - (col + col_count - diagonal_from) // col_count
+    for kind in range(row_count):
+        y = rows_by[kind]
+        if kind > 0:
+            for p in range(slots):
+                swap_arrival(kind, p).wait_recv()
+        for p in range(slots):
+            partner = p * (1 - flip) + (slots - 1 - p) * flip
+            for c in range(col_count):
+                some = pl.ds(pl.multiple_of(y * a_local + c * group, group), group)
+                other = swap_in[y, partner, pl.ds(c * group, group), :]
+                both = resid[p, some, :] + other.astype(jnp.float32)
+                rsym[kind, c, p] = both.astype(jnp.bfloat16)
+        for step in range(1, col_count):
+            back_copy(kind, step).start()
+        out_ref[col, y] = rsym[kind, col]
+    for kind in range(row_count):
+        for step in range(1, col_count):
+            back_arrival(kind, step).wait_recv()
 
     for q in range(q_count):
         for step in range(1, row_count):
@@ -277,33 +425,18 @@
                     ring_copy(way, q, half, hop).wait_send()
     for step in range(1, col_count):
         tile_copy(step).wait_send()
+        s_copy(step).wait_send()
+        for kind in range(row_count):
+            back_copy(kind, step).wait_send()
     for kind in range(3):
-        slab_copy(kind).wait_send()
-
-
-def resid_kernel(ladder_ref, s_ref, resid_ref, swap_ref):
-    col_count, slots, row_count, group, a_local = s_ref.shape
+        for step in range(col_count):
+            slab_copy(kind, step).wait_send()
+        for p in range(slots):
+            swap_copy(kind + 1, p).wait_send()
     for p in range(slots):
-        for y in range(row_count):
-            for c in range(col_count):
-                some = pl.ds(y * a_local + c * group, group)
-                resid_ref[p, some, :] = s_ref[c, p, y].astype(jnp.float32) + ladder_ref[
-                    p, some, :
-                ].astype(jnp.float32)
-            swap_ref[y, p] = resid_ref[p, pl.ds(y * a_local, a_local), :].T.astype(jnp.bfloat16)
-
-
-def add_kernel(diagonal_from, resid_ref, swap_ref, out_ref):
-    col_count, slots, row_count, group, a_local = out_ref.shape
-    flip = (lax.axis_index("col") < diagonal_from).astype(jnp.int32)
-    for p in range(slots):
-        partner = p * (1 - flip) + (slots - 1 - p) * flip
-        for y in range(row_count):
-            for c in range(col_count):
-                some = pl.ds(y * a_local + c * group, group)
-                other = swap_ref[y, partner, pl.ds(c * group, group), :]
-                both = resid_ref[p, some, :] + other.astype(jnp.float32)
-                out_ref[c, p, y] = both.astype(jnp.bfloat16)
+        core_copy(p, 0).wait_send()
+        core_copy(p, 1).wait_send()
+        across_copy(p).wait_send()
 
 
 def update_kernel(table, amps_ref, rsym_ref, mask_ref, occ_ref, vir_b_ref, vir_a_ref, out_ref, rows):
@@ -311,7 +444,7 @@
     half_len = a_local // mask_ref.shape[0]
     for owner, pairs in enumerate(table):
         for slot, pair in enumerate(pairs):
-            one = rsym_ref[owner, slot].reshape(LANES, a_local).astype(jnp.float32)
+            one = rsym_ref[owner, :, slot].reshape(LANES, a_local).astype(jnp.float32)
             rows[pair] = one.T
     known = occ_ref[...] - vir_b_ref[...]
     for half in range(mask_ref.shape[0]):
@@ -374,25 +507,44 @@
     )(amps, source, mask)
     sem = pltpu.SemaphoreType.DMA
     ring_sems = sem((2, share, 2, col_count // 2))
-    partial = pl.pallas_call(
-        ladder_kernel,
-        out_shape=jax.ShapeDtypeStruct((row_count, slots, virt, a_local), bf16),
-        in_specs=[pl.BlockSpec(memory_space=VMEM), pl.BlockSpec(memory_space=pl.ANY)],
+    back = (col_count, row_count, slots, group, a_local)
+    rsym = pl.pallas_call(
+        functools.partial(ladder_kernel, occ_count * (occ_count - 1) // 2),
+        out_shape=jax.ShapeDtypeStruct(back, bf16),
+        in_specs=[pl.BlockSpec(memory_space=VMEM)] + [pl.BlockSpec(memory_space=pl.ANY)] * 2,
         out_specs=pl.BlockSpec(memory_space=VMEM),
         scratch_shapes=[
             VMEM((row_count, slots, row_count, col_count, group, a_local), bf16),
             VMEM((share, row_count, col_count, group, virt), bf16),
             VMEM((virt, virt), bf16),
             VMEM((slots, virt, virt), f32),
-            sem((share + 1,)),
+            VMEM((row_count, slots, virt, a_local), bf16),
+            VMEM((row_count // 2, slots, virt, a_local), bf16),
+            VMEM((slots, virt, a_local), bf16),
+            VMEM(block, bf16),
+            VMEM((slots, virt, a_local), f32),
+            VMEM((row_count - 1, slots, a_local, a_local), bf16),
+            VMEM((row_count, slots, a_local, a_local), bf16),
+            VMEM((row_count, col_count, slots, group, a_local), bf16),
+            sem((share + 2,)),
             sem((share, row_count - 1)),
             sem((share, row_count - 1)),
             sem((col_count - 1,)),
             sem((col_count - 1,)),
-            sem((3,)),
-            sem((3,)),
+            sem((3, col_count)),
+            sem((3, col_count)),
             ring_sems,
             ring_sems,
+            sem((col_count - 1,)),
+            sem((col_count - 1,)),
+            sem((slots, 2)),
+            sem((slots, 2)),
+            sem((slots,)),
+            sem((slots,)),
+            sem((row_count - 1, slots)),
+            sem((row_count - 1, slots)),
+            sem((row_count, col_count - 1)),
+            sem((row_count, col_count - 1)),
         ],
         compiler_params=pltpu.CompilerParams(
             vmem_limit_bytes=56 * 1024 * 1024, collective_id=0, has_side_effects=True
@@ -401,32 +553,7 @@
             flops=4 * share * slots * virt**3, bytes_accessed=16 * 1024 * 1024, transcendentals=0
         ),
         name="ladder",
-    )(tm_blocks, factors.reshape(row_count, share, group, virt))
-    s_mine = lax.all_to_all(s_blocks, "col", split_axis=0, concat_axis=0, tiled=True)
-
-    ladder = lax.psum_scatter(partial, "row", scatter_dimension=0, tiled=True)
-    ladder = ladder.reshape(slots, virt, a_local)
-    resid, swap = pl.pallas_call(
-        resid_kernel,
-        out_shape=[
-            jax.ShapeDtypeStruct((slots, virt, a_local), f32),
-            jax.ShapeDtypeStruct((row_count, slots, a_local, a_local), bf16),
-        ],
-        in_specs=whole(2),
-        out_specs=whole(2),
-        compiler_params=params(),
-        name="resid",
-    )(ladder, s_mine)
-    swapped = lax.all_to_all(swap, "row", split_axis=0, concat_axis=0, tiled=True)
-    rsym = pl.pallas_call(
-        functools.partial(add_kernel, occ_count * (occ_count - 1) // 2),
-        out_shape=jax.ShapeDtypeStruct(block, bf16),
-        in_specs=whole(2),
-        out_specs=whole(1)[0],
-        compiler_params=params(),
-        name="add_swapped",
-    )(resid, swapped)
-    rsym = lax.all_to_all(rsym, "col", split_axis=0, concat_axis=0, tiled=True)
+    )(tm_blocks, s_blocks, factors.reshape(row_count, share, group, virt))
     new = pl.pallas_call(
         functools.partial(update_kernel, table),
         out_shape=jax.ShapeDtypeStruct((pair_count, a_local * b_local), bf16),

time: 274 us -> 200 us (0.73)
  blocking collectives: 45.2 us -> 0 us
  waiting for transfers between devices: 41.6 us -> 0 us
  Pallas kernels: 161 us -> 195 us
  between operations: 13.4 us -> 0.03 us
  starting transfers between devices: 5.53 us -> 0 us
    all_to_all x2 -> x0, blocking collectives: 45.2 us -> none  [the longest x1 26.3 us: fast_shards(): lax.all_to_all(s_blocks, 'col', split_axis=0, concat_axis=0, tiled=True)]
    pallas_call x3 -> x1, Pallas kernels: 150 us -> 184 us  [fast_shards(): pl.pallas_call(functools.partial(ladder_kernel, occ_count * (occ_count -...]
    all_to_all x1 -> x0, waiting for transfers between devices: 23.5 us -> none  [fast_shards(): rsym = lax.all_to_all(rsym, 'col', split_axis=0, concat_axis=0, tiled=True)]
    reduce_scatter x1 -> x0, waiting for transfers between devices: 18.1 us -> none  [fast_shards(): ladder = lax.psum_scatter(partial, 'row', scatter_dimension=0, tiled=True)]
    all_to_all x1 -> x0, starting transfers between devices: 5.53 us -> none  [fast_shards(): rsym = lax.all_to_all(rsym, 'col', split_axis=0, concat_axis=0, tiled=True)]
  transfers between devices with their start and end apart: 2 -> 0, of which waited for: 2 -> 0; matrix products, arithmetic and copies ran while one was open for 1% -> 0% of each run, Pallas kernels for 0% -> 0%
where the time goes in v4:
time: 200 us
  Pallas kernels  195 us (98%)
  local copies, waits for them, and re-layouts  4.31 us (2%)
    pallas_call x1, Pallas kernels, fast_shards(): pl.pallas_call(functools.partial(ladder_kernel, occ_count * (occ_count -...  184 us
    pallas_call x1, Pallas kernels, fast_shards(): pl.pallas_call(functools.partial(pack_kernel, table), out_shape=[jax.Shap...  6.82 us
    pallas_call x1, Pallas kernels, fast_shards(): pl.pallas_call(functools.partial(update_kernel, table), out_shape=jax.Sha...  4.68 us

profile of v4, /device:TPU:0, one launch (start us, length us, event | category | flops | bytes accessed | tf_op | source)
XLA Modules:
  0.0 199.7 jit_solution(8352492944620385236)
XLA Ops:
  0.0 0.0 copy-start
  0.0 0.8 copy-done
  0.8 0.1 copy.9
  0.9 0.1 broadcast_in_dim.10
  1.0 0.7 reshape.52.mask_ref
  1.7 6.8 %pack_tiles.1 = (bf16[8,2,4,32,256]{4,3,2,1,0:T(8,128)(2,1)}, bf16[8,2,4,32,256]{4,3,2,1,0:T(8,128)(2,1)}) custom-call(bf16[16,32768]{1,0:T(8,128)(2,1)} %bitcast.8, bf16[16,32768]{1,0:T(8,128)(2,1)} %bitcast.10, f32[2,16,128]{2,1,0:T(8,128)} %reshape.52.mask_ref), custom_call_target="tpu_custom_call" | custom-call | tf_op jit(solution)/shard_map/pack_tiles/pallas_call | solution.py:499
  8.5 0.0 copy-start.2
  8.5 183.8 %ladder.1.rsym_ref = bf16[8,4,2,32,256]{4,3,2,1,0:T(8,128)(2,1)} custom-call(bf16[8,2,4,32,256]{4,3,2,1,0:T(8,128)(2,1)} %get-tuple-element.7.tm_ref, bf16[8,2,4,32,256]{4,3,2,1,0:T(8,128)(2,1)} %get-tuple-element.8.s_ref, bf16[4,4,32,1024]{3,2,1,0:T(8,128)(2,1)} %bitcast.13), custom_call_target="tpu_custom_call" | custom-call | flops 34359738368 | bytes 16777216 | tf_op jit(solution)/shard_map/ladder/pallas_call | solution.py:511
  192.3 0.0 copy-start.1
  192.3 0.7 copy-done.1
  193.0 0.1 reshape.54
  193.1 0.6 reshape.55.vir_b_ref
  193.7 0.6 dynamic_slice.15.vir_a_ref
  194.3 0.0 copy-done.2
  194.3 0.1 broadcast_add_fusion
  194.4 0.7 add.44.occ_ref
  195.0 4.7 %update.1 = bf16[16,32768]{1,0:T(8,128)(2,1)} custom-call(bf16[16,32768]{1,0:T(8,128)(2,1)} %bitcast.9, bf16[8,4,2,32,256]{4,3,2,1,0:T(8,128)(2,1)} %ladder.1.rsym_ref, f32[2,16,128]{2,1,0:T(8,128)} %reshape.52.mask_ref, f32[16,1]{1,0:T(8,128)} %add.44.occ_ref, f32[1,128]{1,0:T(1,128)} %reshape.55.vir_b_ref, f32[256]{0:T(256)} %dynamic_slice.15.vir_a_ref), custom_call_target="tpu_custom_call" | custom-call | tf_op jit(solution)/shard_map/update/pallas_call | solution.py:557
  (3 shorter events, 0.0 us)
Async XLA Ops:
  0.0 0.8 copy-start
  8.5 185.8 %copy-start.2 = (f32[4]{0:T(128)S(1)}, f32[4]{0:T(128)}, u32[]{:S(2)}) copy-start(f32[4]{0:T(128)} %param.10) | copy-start | bytes 52
  192.3 0.7 copy-start.1

commit v5 on v4

--- a/solution.py
+++ b/solution.py
@@ -25,29 +25,24 @@
     return [pl.BlockSpec(memory_space=VMEM)] * count
 
 
-def pack_kernel(table, amps_ref, source_ref, mask_ref, tm_ref, s_ref, rows):
-    pair_count, a_local = rows.shape[0], rows.shape[1]
-    groups, group = tm_ref.shape[2], tm_ref.shape[3]
-    half_len = a_local // mask_ref.shape[0]
-
-    def turn(in_ref, out_ref, masked):
-        for half in range(mask_ref.shape[0]):
-
-            @pl.loop(0, half_len, unroll=8)
-            def _(step):
-                x = half * half_len + step
-                one = in_ref[:, pl.ds(pl.multiple_of(x * LANES, LANES), LANES)].astype(jnp.float32)
-                if masked:
-                    one = one * mask_ref[half]
-                rows[:, x, :] = one
-
-        for dest, pairs in enumerate(table):
-            for slot, pair in enumerate(pairs):
-                turned = rows[pair].T.astype(jnp.bfloat16)
-                out_ref[dest, slot] = turned.reshape(groups, group, a_local)
-
-    turn(amps_ref, tm_ref, True)
-    turn(source_ref, s_ref, False)
+def turn(table, in_ref, out_ref, rows, mask_ref, halves):
+    a_local = rows.shape[1]
+    groups, group = out_ref.shape[2], out_ref.shape[3]
+    half_len = a_local // halves
+    for half in range(halves):
+
+        @pl.loop(0, half_len, unroll=8)
+        def _(step):
+            x = half * half_len + step
+            one = in_ref[:, pl.ds(pl.multiple_of(x * LANES, LANES), LANES)].astype(jnp.float32)
+            if mask_ref is not None:
+                one = one * mask_ref[half]
+            rows[:, x, :] = one
+
+    for dest, pairs in enumerate(table):
+        for slot, pair in enumerate(pairs):
+            turned = rows[pair].T.astype(jnp.bfloat16)
+            out_ref[dest, slot] = turned.reshape(groups, group, a_local)
 
 
 def ring_column(position, count):
@@ -57,11 +52,16 @@
 
 
 def ladder_kernel(
+    table,
     diagonal_from,
+    amps_ref,
+    source_ref,
+    mask_ref,
+    factors_ref,
+    out_ref,
+    rows,
     tm_ref,
     s_ref,
-    factors_ref,
-    out_ref,
     t_all,
     b_all,
     inner,
@@ -96,6 +96,9 @@
 ):
     q_count, row_count, col_count, group, virt = b_all.shape
     slots, a_local = t_all.shape[1], t_all.shape[5]
+    block = 512
+    blocks = virt // block
+    rows_per = block // a_local
     row, col = lax.axis_index("row"), lax.axis_index("col")
     sibling = row + 1 - 2 * (row % 2)
     across = (row + 2) % row_count
@@ -203,13 +206,12 @@
             for way in range(2):
                 ring_copy(way, q, half, 0).start()
 
-    def ring_step(q, hop):
-        for half in range(2):
-            for way in range(2):
-                if hop < hops(q, way):
-                    ring_arrival(way, q, half, hop).wait_recv()
-                    if hop + 1 < hops(q, way):
-                        ring_copy(way, q, half, hop + 1).start()
+    def ring_step(q, half, hop):
+        for way in range(2):
+            if hop < hops(q, way):
+                ring_arrival(way, q, half, hop).wait_recv()
+                if hop + 1 < hops(q, way):
+                    ring_copy(way, q, half, hop + 1).start()
 
     def s_copy(step):
         to_col = (col + step) % col_count
@@ -221,27 +223,31 @@
         here = s_all.at[from_col]
         return remote(here, here, s_send.at[step - 1], s_recv.at[step - 1], {"col": from_col})
 
-    def core_copy(p, near):
-        source = part.at[sibling if near else diagonal, p]
-        dest = core_in.at[chip if near else 1 - chip, p]
-        return remote(source, dest, core_send.at[p, near], core_recv.at[p, near], {"row": sibling})
-
-    def core_arrival(p, near):
-        here = core_in.at[chip if near else 1 - chip, p]
-        return remote(here, here, core_send.at[p, near], core_recv.at[p, near], {"row": sibling})
-
-    def across_copy(p):
-        sems = across_send.at[p], across_recv.at[p]
-        return remote(part.at[across, p], across_in.at[p], *sems, {"row": across})
-
-    def across_arrival(p):
-        here = across_in.at[p]
-        return remote(here, here, across_send.at[p], across_recv.at[p], {"row": across})
-
-    def send_across(p):
-        core_arrival(p, 0).wait_recv()
-
-        @pl.loop(0, row_count)
+    def core_copy(p, m, near):
+        some = pl.ds(m * block, block)
+        source = part.at[sibling if near else diagonal, p, some]
+        dest = core_in.at[chip if near else 1 - chip, p, some]
+        sems = core_send.at[p, m, near], core_recv.at[p, m, near]
+        return remote(source, dest, *sems, {"row": sibling})
+
+    def core_arrival(p, m, near):
+        here = core_in.at[chip if near else 1 - chip, p, pl.ds(m * block, block)]
+        sems = core_send.at[p, m, near], core_recv.at[p, m, near]
+        return remote(here, here, *sems, {"row": sibling})
+
+    def across_copy(p, m):
+        some = pl.ds(m * block, block)
+        sems = across_send.at[p, m], across_recv.at[p, m]
+        return remote(part.at[across, p, some], across_in.at[p, some], *sems, {"row": across})
+
+    def across_arrival(p, m):
+        here = across_in.at[p, pl.ds(m * block, block)]
+        return remote(here, here, across_send.at[p, m], across_recv.at[p, m], {"row": across})
+
+    def send_across(p, m):
+        core_arrival(p, m, 0).wait_recv()
+
+        @pl.loop(m * rows_per, (m + 1) * rows_per)
         def _(y):
             some = pl.ds(pl.multiple_of(y * a_local, a_local), a_local)
             both = part[across, p, some, :].astype(jnp.float32) + core_in[
@@ -249,7 +255,7 @@
             ].astype(jnp.float32)
             part[across, p, some, :] = both.astype(jnp.bfloat16)
 
-        across_copy(p).start()
+        across_copy(p, m).start()
 
     def swap_copy(kind, p):
         sems = swap_send.at[kind - 1, p], swap_recv.at[kind - 1, p]
@@ -280,43 +286,46 @@
     near_tile = pltpu.make_async_copy(
         tm_ref.at[col], t_all.at[row, :, :, col], near_sem.at[q_count]
     )
-    near_tile.start()
-    for step in range(1, col_count):
-        tile_copy(step).start()
     for q in range(q_count):
         near_share[q].start()
         for step in range(1, row_count):
             share_copy(q, step).start()
 
-    block = 512
-    blocks = virt // block
-    rows_per = block // a_local
+    halves = mask_ref.shape[0]
+    turn(table, amps_ref, tm_ref, rows, mask_ref, halves)
+    near_tile.start()
+    for step in range(1, col_count):
+        tile_copy(step).start()
+
     stagger = col_count // 4
 
-    def ring_slot(slot):
+    def ring_slot(slot, half):
         q = slot // stagger
-        if (slot + 1) % stagger == 0 and q + 1 < q_count:
+        if half == 0 and (slot + 1) % stagger == 0 and q + 1 < q_count:
             ring_begin(q + 1)
         if q < q_count:
-            ring_step(q, slot % stagger)
+            ring_step(q, half, slot % stagger)
         if q > 0:
-            ring_step(q - 1, stagger + slot % stagger)
+            ring_step(q - 1, half, stagger + slot % stagger)
 
     near_tile.wait()
     slab_copy(0, 0).start()
     slab_copy(1, 0).start()
     ring_begin(0)
+    turn(table, source_ref, s_ref, rows, None, halves)
     for step in range(1, col_count):
         tile_arrival(step).wait_recv()
         slab_copy(0, step).start()
         slab_copy(1, step).start()
     for slot in range(stagger):
-        ring_slot(slot)
+        ring_slot(slot, 0)
+        ring_slot(slot, 1)
     for step in range(col_count):
         slab_arrival(1, step).wait_recv()
         slab_copy(2, step).start()
     for slot in range(stagger, 2 * stagger):
-        ring_slot(slot)
+        ring_slot(slot, 0)
+        ring_slot(slot, 1)
     for step in range(col_count):
         slab_arrival(0, step).wait_recv()
         slab_arrival(2, step).wait_recv()
@@ -338,47 +347,55 @@
                     pl.ds(pl.multiple_of(n * a_local, a_local), a_local),
                 ] = jnp.dot(left, right, preferred_element_type=jnp.float32).astype(jnp.bfloat16)
 
-            if q == q_count - 1 and p > 0:
-                send_across(p - 1)
-
-            @pl.loop(0, blocks * blocks)
-            def _(step):
-                m, n = step // blocks, step % blocks
-                some = pl.ds(pl.multiple_of(m * block, block), block)
-                cols = pl.ds(pl.multiple_of(n * block, block), block)
-                right = b_all[q, pl.ds(n * rows_per, rows_per)].reshape(block, virt)
-                product = lax.dot_general(
-                    inner[some, :],
-                    right,
-                    (((1,), (1,)), ((), ())),
-                    preferred_element_type=jnp.float32,
-                )
-                if q > 0:
-                    product = product + total[p, some, cols]
-                if q == q_count - 1:
-                    for k in range(rows_per):
-                        part[n * rows_per + k, p, some, :] = product[
-                            :, k * a_local : (k + 1) * a_local
-                        ].astype(jnp.bfloat16)
-                else:
-                    total[p, some, cols] = product
-
             if q + 1 < q_count:
                 for slot in range(p * stagger // slots, (p + 1) * stagger // slots):
-                    ring_slot((q + 2) * stagger + slot)
-            else:
-                core_copy(p, 0).start()
-                core_copy(p, 1).start()
-
-    send_across(slots - 1)
+                    ring_slot((q + 2) * stagger + slot, 0)
+            elif p > 0:
+                send_across(p - 1, blocks - 1)
+
+            for m in range(blocks):
+                some = slice(m * block, (m + 1) * block)
+
+                @pl.loop(0, blocks)
+                def _(n):
+                    cols = pl.ds(pl.multiple_of(n * block, block), block)
+                    right = b_all[q, pl.ds(n * rows_per, rows_per)].reshape(block, virt)
+                    product = lax.dot_general(
+                        inner[some, :],
+                        right,
+                        (((1,), (1,)), ((), ())),
+                        preferred_element_type=jnp.float32,
+                    )
+                    if q > 0:
+                        product = product + total[p, some, cols]
+                    if q == q_count - 1:
+                        for k in range(rows_per):
+                            part[n * rows_per + k, p, some, :] = product[
+                                :, k * a_local : (k + 1) * a_local
+                            ].astype(jnp.bfloat16)
+                    else:
+                        total[p, some, cols] = product
+
+                if q == q_count - 1:
+                    core_copy(p, m, 0).start()
+                    core_copy(p, m, 1).start()
+                    if m > 0:
+                        send_across(p, m - 1)
+
+            if q + 1 < q_count:
+                for slot in range(p * stagger // slots, (p + 1) * stagger // slots):
+                    ring_slot((q + 2) * stagger + slot, 1)
+
+    send_across(slots - 1, blocks - 1)
     near_s.wait()
     for step in range(1, col_count):
         s_arrival(step).wait_recv()
 
     for p in range(slots):
-        core_arrival(p, 1).wait_recv()
-        across_arrival(p).wait_recv()
         for y in range(row_count):
+            if y % rows_per == 0:
+                core_arrival(p, y // rows_per, 1).wait_recv()
+                across_arrival(p, y // rows_per).wait_recv()
             for c in range(col_count):
                 some = pl.ds(y * a_local + c * group, group)
                 resid[p, some, :] = (
@@ -434,9 +451,10 @@
         for p in range(slots):
             swap_copy(kind + 1, p).wait_send()
     for p in range(slots):
-        core_copy(p, 0).wait_send()
-        core_copy(p, 1).wait_send()
-        across_copy(p).wait_send()
+        for m in range(blocks):
+            core_copy(p, m, 0).wait_send()
+            core_copy(p, m, 1).wait_send()
+            across_copy(p, m).wait_send()
 
 
 def update_kernel(table, amps_ref, rsym_ref, mask_ref, occ_ref, vir_b_ref, vir_a_ref, out_ref, rows):
@@ -496,24 +514,18 @@
     ).reshape(1, b_local)
 
     block = (col_count, slots, row_count, group, a_local)
-    tm_blocks, s_blocks = pl.pallas_call(
-        functools.partial(pack_kernel, table),
-        out_shape=[jax.ShapeDtypeStruct(block, bf16)] * 2,
-        in_specs=whole(3),
-        out_specs=whole(2),
-        scratch_shapes=[VMEM((pair_count, a_local, LANES), f32)],
-        compiler_params=params(),
-        name="pack_tiles",
-    )(amps, source, mask)
     sem = pltpu.SemaphoreType.DMA
     ring_sems = sem((2, share, 2, col_count // 2))
     back = (col_count, row_count, slots, group, a_local)
     rsym = pl.pallas_call(
-        functools.partial(ladder_kernel, occ_count * (occ_count - 1) // 2),
+        functools.partial(ladder_kernel, table, occ_count * (occ_count - 1) // 2),
         out_shape=jax.ShapeDtypeStruct(back, bf16),
-        in_specs=[pl.BlockSpec(memory_space=VMEM)] + [pl.BlockSpec(memory_space=pl.ANY)] * 2,
+        in_specs=whole(3) + [pl.BlockSpec(memory_space=pl.ANY)],
         out_specs=pl.BlockSpec(memory_space=VMEM),
         scratch_shapes=[
+            VMEM((pair_count, a_local, LANES), f32),
+            VMEM(block, bf16),
+            VMEM(block, bf16),
             VMEM((row_count, slots, row_count, col_count, group, a_local), bf16),
             VMEM((share, row_count, col_count, group, virt), bf16),
             VMEM((virt, virt), bf16),
@@ -537,10 +549,10 @@
             ring_sems,
             sem((col_count - 1,)),
             sem((col_count - 1,)),
-            sem((slots, 2)),
-            sem((slots, 2)),
-            sem((slots,)),
-            sem((slots,)),
+            sem((slots, virt // 512, 2)),
+            sem((slots, virt // 512, 2)),
+            sem((slots, virt // 512)),
+            sem((slots, virt // 512)),
             sem((row_count - 1, slots)),
             sem((row_count - 1, slots)),
             sem((row_count, col_count - 1)),
@@ -553,7 +565,7 @@
             flops=4 * share * slots * virt**3, bytes_accessed=16 * 1024 * 1024, transcendentals=0
         ),
         name="ladder",
-    )(tm_blocks, s_blocks, factors.reshape(row_count, share, group, virt))
+    )(amps, source, mask, factors.reshape(row_count, share, group, virt))
     new = pl.pallas_call(
         functools.partial(update_kernel, table),
         out_shape=jax.ShapeDtypeStruct((pair_count, a_local * b_local), bf16),

time: 200 us -> 188 us (0.940)
  Pallas kernels: 195 us -> 184 us
    pallas_call x2 -> x1, Pallas kernels: 191 us -> 180 us  [fast_shards(): pl.pallas_call(functools.partial(ladder_kernel, table, occ_count * (occ_c...]
where the time goes in v5:
time: 188 us
  Pallas kernels  184 us (98%)
  local copies, waits for them, and re-layouts  3.57 us (2%)
    pallas_call x1, Pallas kernels, fast_shards(): pl.pallas_call(functools.partial(ladder_kernel, table, occ_count * (occ_c...  180 us
    pallas_call x1, Pallas kernels, fast_shards(): pl.pallas_call(functools.partial(update_kernel, table), out_shape=jax.Sha...  4.69 us

profile of v5, /device:TPU:0, one launch (start us, length us, event | category | flops | bytes accessed | tf_op | source)
XLA Modules:
  0.0 188.0 jit_solution(2265835457356442001)
XLA Ops:
  0.0 0.0 copy-start
  0.0 0.0 copy-start.1
  0.0 0.7 copy-done.1
  0.7 0.0 copy-start.2
  0.7 0.6 dynamic_slice.15.vir_a_ref
  1.3 0.0 copy-done.2
  1.4 0.1 broadcast_add_fusion
  1.4 0.7 add.44.occ_ref
  2.1 0.0 copy-done
  2.1 0.1 copy.9
  2.2 0.1 reshape.54
  2.3 0.6 reshape.55.vir_b_ref
  2.9 0.1 broadcast_in_dim.10
  3.0 0.7 reshape.52.mask_ref
  3.7 179.6 %ladder.1.rsym_ref = bf16[8,4,2,32,256]{4,3,2,1,0:T(8,128)(2,1)} custom-call(bf16[16,32768]{1,0:T(8,128)(2,1)} %bitcast.8, bf16[16,32768]{1,0:T(8,128)(2,1)} %bitcast.12, f32[2,16,128]{2,1,0:T(8,128)} %reshape.52.mask_ref, bf16[4,4,32,1024]{3,2,1,0:T(8,128)(2,1)} %bitcast.13), custom_call_target="tpu_custom_call" | custom-call | flops 34359738368 | bytes 16777216 | tf_op jit(solution)/shard_map/ladder/pallas_call | solution.py:520
  183.3 4.7 %update.1 = bf16[16,32768]{1,0:T(8,128)(2,1)} custom-call(bf16[16,32768]{1,0:T(8,128)(2,1)} %bitcast.9, bf16[8,4,2,32,256]{4,3,2,1,0:T(8,128)(2,1)} %ladder.1.rsym_ref, f32[2,16,128]{2,1,0:T(8,128)} %reshape.52.mask_ref, f32[16,1]{1,0:T(8,128)} %add.44.occ_ref, f32[1,128]{1,0:T(1,128)} %reshape.55.vir_b_ref, f32[256]{0:T(256)} %dynamic_slice.15.vir_a_ref), custom_call_target="tpu_custom_call" | custom-call | tf_op jit(solution)/shard_map/update/pallas_call | solution.py:569
  (3 shorter events, 0.0 us)
Async XLA Ops:
  0.0 2.1 %copy-start = (s32[16,8,8]{0,2,1:T(8,128)S(1)}, s32[16,8,8]{0,2,1:T(8,128)}, u32[]{:S(2)}) copy-start(s32[16,8,8]{0,2,1:T(8,128)} %param.9) | copy-start | bytes 12292
  0.0 0.7 copy-start.1
  0.7 0.7 copy-start.2

commit v6 on v5

--- a/solution.py
+++ b/solution.py
@@ -56,9 +56,10 @@
     diagonal_from,
     amps_ref,
     source_ref,
-    mask_ref,
+    screen_ref,
     factors_ref,
     out_ref,
+    mask_ref,
     rows,
     tm_ref,
     s_ref,
@@ -178,8 +179,8 @@
         sems = slab_send.at[kind, step], slab_recv.at[kind, step]
         return remote(slab, slab, *sems, {"row": sibling})
 
-    def hops(q, way):
-        return col_count // 2 - (q + way) % 2
+    def hops(half, way):
+        return col_count // 2 - (half + way) % 2
 
     def ring_block(q, half, position):
         return b_all.at[q, pl.ds(half * half_rows, half_rows), ring_column(position, col_count)]
@@ -208,9 +209,9 @@
 
     def ring_step(q, half, hop):
         for way in range(2):
-            if hop < hops(q, way):
+            if hop < hops(half, way):
                 ring_arrival(way, q, half, hop).wait_recv()
-                if hop + 1 < hops(q, way):
+                if hop + 1 < hops(half, way):
                     ring_copy(way, q, half, hop + 1).start()
 
     def s_copy(step):
@@ -292,6 +293,15 @@
             share_copy(q, step).start()
 
     halves = mask_ref.shape[0]
+    block_size = virt // screen_ref.shape[0]
+    lane_group = lax.broadcasted_iota(jnp.int32, (1, LANES), 1) // group
+    for half in range(halves):
+        for pair in range(mask_ref.shape[1]):
+            kept = jnp.zeros((1, LANES), jnp.float32)
+            for y in range(row_count):
+                one = screen_ref[row * halves + half, y * halves + col * group // block_size, pair]
+                kept = jnp.where(lane_group == y, one.astype(jnp.float32), kept)
+            mask_ref[half, pair : pair + 1, :] = kept
     turn(table, amps_ref, tm_ref, rows, mask_ref, halves)
     near_tile.start()
     for step in range(1, col_count):
@@ -438,7 +448,7 @@
             share_copy(q, step).wait_send()
         for half in range(2):
             for way in range(2):
-                for hop in range(hops(q, way)):
+                for hop in range(hops(half, way)):
                     ring_copy(way, q, half, hop).wait_send()
     for step in range(1, col_count):
         tile_copy(step).wait_send()
@@ -457,21 +467,36 @@
             across_copy(p, m).wait_send()
 
 
-def update_kernel(table, amps_ref, rsym_ref, mask_ref, occ_ref, vir_b_ref, vir_a_ref, out_ref, rows):
+def update_kernel(table, amps_ref, rsym_ref, mask_ref, occ_ref, vir_ref, out_ref, rows):
     pair_count, a_local = rows.shape[0], rows.shape[1]
     half_len = a_local // mask_ref.shape[0]
     for owner, pairs in enumerate(table):
         for slot, pair in enumerate(pairs):
             one = rsym_ref[owner, :, slot].reshape(LANES, a_local).astype(jnp.float32)
             rows[pair] = one.T
-    known = occ_ref[...] - vir_b_ref[...]
+    col_count, row_count, group = rsym_ref.shape[0], rsym_ref.shape[1], rsym_ref.shape[3]
+    occ_count = occ_ref.shape[0]
+    row, col = lax.axis_index("row"), lax.axis_index("col")
+    lane = lax.broadcasted_iota(jnp.int32, (8, LANES), 1)
+    pair_of = lax.broadcasted_iota(jnp.int32, (pair_count, LANES), 0)
+
+    def with_lane(y, vir_b):
+        b = y // group * a_local + col * group + y % group
+        return jnp.where(lane == y, vir_ref[b], vir_b)
+
+    vir_b = lax.fori_loop(0, LANES, with_lane, jnp.zeros((8, LANES), jnp.float32), unroll=8)
+    known = jnp.zeros((pair_count, LANES), jnp.float32)
+    for pair in range(pair_count):
+        occ_pair = occ_ref[pair // occ_count] + occ_ref[pair % occ_count]
+        known = jnp.where(pair_of == pair, occ_pair, known)
+    known = known - vir_b[:1]
     for half in range(mask_ref.shape[0]):
 
         @pl.loop(0, half_len, unroll=8)
         def _(step):
             x = half * half_len + step
             lanes = pl.ds(pl.multiple_of(x * LANES, LANES), LANES)
-            denom = known - vir_a_ref[x]
+            denom = known - vir_ref[row * a_local + x]
             new = mask_ref[half] * (amps_ref[:, lanes].astype(jnp.float32) + rows[:, x, :] / denom)
             out_ref[:, lanes] = new.astype(jnp.bfloat16)
 
@@ -483,8 +508,6 @@
 def fast_shards(amps, source, factors, screen, occ_energy, vir_energy):
     row_count = lax.axis_size("row")
     col_count = lax.axis_size("col")
-    row_id = lax.axis_index("row")
-    col_id = lax.axis_index("col")
     pair_count = amps.shape[2]
     aux_count, group, virt = factors.shape
     a_local = col_count * group
@@ -493,7 +516,6 @@
     block_count = screen.shape[1]
     block_size = virt // block_count
     halves = a_local // block_size
-    per_y = block_count // row_count
     slots = pair_count // col_count
     share = aux_count // row_count
     table = pair_table(occ_count)
@@ -501,27 +523,19 @@
 
     amps = amps.reshape(pair_count, a_local * b_local)
     source = source.reshape(pair_count, a_local * b_local)
-    mine = lax.dynamic_slice_in_dim(screen, row_id * halves, halves, 1)
-    mine = mine.reshape(pair_count, halves, row_count, per_y)
-    mine = lax.dynamic_slice_in_dim(mine, col_id * group // block_size, 1, 3)
-    mask = jnp.broadcast_to(
-        mine.transpose(1, 0, 2, 3).astype(f32), (halves, pair_count, row_count, group)
-    ).reshape(halves, pair_count, b_local)
-    occ_pair = (occ_energy[:, None] + occ_energy[None, :]).reshape(pair_count, 1)
-    vir_a = lax.dynamic_slice_in_dim(vir_energy, row_id * a_local, a_local)
-    vir_b = lax.dynamic_slice_in_dim(
-        vir_energy.reshape(row_count, col_count, group), col_id, 1, 1
-    ).reshape(1, b_local)
-
     block = (col_count, slots, row_count, group, a_local)
     sem = pltpu.SemaphoreType.DMA
     ring_sems = sem((2, share, 2, col_count // 2))
     back = (col_count, row_count, slots, group, a_local)
-    rsym = pl.pallas_call(
+    rsym, mask = pl.pallas_call(
         functools.partial(ladder_kernel, table, occ_count * (occ_count - 1) // 2),
-        out_shape=jax.ShapeDtypeStruct(back, bf16),
-        in_specs=whole(3) + [pl.BlockSpec(memory_space=pl.ANY)],
-        out_specs=pl.BlockSpec(memory_space=VMEM),
+        out_shape=[
+            jax.ShapeDtypeStruct(back, bf16),
+            jax.ShapeDtypeStruct((halves, pair_count, b_local), f32),
+        ],
+        in_specs=whole(2)
+        + [pl.BlockSpec(memory_space=pltpu.SMEM), pl.BlockSpec(memory_space=pl.ANY)],
+        out_specs=whole(2),
         scratch_shapes=[
             VMEM((pair_count, a_local, LANES), f32),
             VMEM(block, bf16),
@@ -565,16 +579,16 @@
             flops=4 * share * slots * virt**3, bytes_accessed=16 * 1024 * 1024, transcendentals=0
         ),
         name="ladder",
-    )(amps, source, mask, factors.reshape(row_count, share, group, virt))
+    )(amps, source, screen.transpose(1, 2, 0), factors.reshape(row_count, share, group, virt))
     new = pl.pallas_call(
         functools.partial(update_kernel, table),
         out_shape=jax.ShapeDtypeStruct((pair_count, a_local * b_local), bf16),
-        in_specs=whole(5) + [pl.BlockSpec(memory_space=pltpu.SMEM)],
+        in_specs=whole(3) + [pl.BlockSpec(memory_space=pltpu.SMEM)] * 2,
         out_specs=whole(1)[0],
         scratch_shapes=[VMEM((pair_count, a_local, LANES), f32)],
         compiler_params=params(),
         name="update",
-    )(amps, rsym, mask, occ_pair, vir_b, vir_a)
+    )(amps, rsym, mask, occ_energy, vir_energy)
     return new.reshape(1, 1, pair_count, a_local * b_local)
 
 

time: 188 us -> 183 us (0.973)
  local copies, waits for them, and re-layouts: 3.57 us -> 0 us
    pallas_call x1, Pallas kernels: 180 us -> 177 us  [fast_shards(): pl.pallas_call(functools.partial(ladder_kernel, table, occ_count * (occ_c...]
where the time goes in v6:
time: 183 us
  Pallas kernels  183 us (100%)
    pallas_call x1, Pallas kernels, fast_shards(): pl.pallas_call(functools.partial(ladder_kernel, table, occ_count * (occ_c...  177 us
    pallas_call x1, Pallas kernels, fast_shards(): pl.pallas_call(functools.partial(update_kernel, table), out_shape=jax.Sha...  5.56 us

profile of v6, /device:TPU:0, one launch (start us, length us, event | category | flops | bytes accessed | tf_op | source)
XLA Modules:
  0.0 182.6 jit_solution(11899858607260779665)
XLA Ops:
  0.0 177.0 %ladder.1 = (bf16[8,4,2,32,256]{4,3,2,1,0:T(8,128)(2,1)}, f32[2,16,128]{2,1,0:T(8,128)}) custom-call(bf16[16,32768]{1,0:T(8,128)(2,1)} %bitcast.5, bf16[16,32768]{1,0:T(8,128)(2,1)} %bitcast.7, s32[8,8,16]{2,1,0:T(8,128)} %bitcast.9, bf16[4,4,32,1024]{3,2,1,0:T(8,128)(2,1)} %bitcast.8), custom_call_target="tpu_custom_call" | custom-call | flops 34359738368 | bytes 16777216 | tf_op jit(solution)/shard_map/ladder/pallas_call | solution.py:530
  177.0 5.6 %update.1 = bf16[16,32768]{1,0:T(8,128)(2,1)} custom-call(bf16[16,32768]{1,0:T(8,128)(2,1)} %bitcast.6, bf16[8,4,2,32,256]{4,3,2,1,0:T(8,128)(2,1)} %get-tuple-element.7.rsym_ref, f32[2,16,128]{2,1,0:T(8,128)} %get-tuple-element.8.mask_ref, f32[4]{0:T(128)} %occ_ref.1, f32[1024]{0:T(1024)} %vir_ref.1), custom_call_target="tpu_custom_call" | custom-call | tf_op jit(solution)/shard_map/update/pallas_call | solution.py:583
